TPU v7x, 512 devices: a whole 4x4x16 slice. The times are simulated.
512 devices in a mesh: dp: 32 (over z, core), rep: 16 (over y, x).
Axes of the slice: x: 4, y: 4, z: 16, core: 2. Of those that a mesh axis runs over, the one named last changes fastest.
Arguments:
- layer_input: bfloat16 [4, 1024, 4096], P(None, ('rep', 'dp')), parts along dimension 1, may hold values from -6 to 6
- queries: bfloat16 [4, 1024, 4096], P(None, ('rep', 'dp')), parts along dimension 1, may hold values from -160 to 160
- new_keys: bfloat16 [4, 1024, 512], P(None, ('rep', 'dp')), parts along dimension 1, may hold values from -8 to 8
- new_values: bfloat16 [4, 1024, 512], P(None, ('rep', 'dp')), parts along dimension 1, may hold values from -6 to 6
- key_cache: bfloat16 [16384, 32, 512], P(('rep', 'dp')), parts along dimension 0, may hold values from -6 to 6
- value_cache: bfloat16 [16384, 32, 512], P(('rep', 'dp')), parts along dimension 0, may hold values from -6 to 6
- norm_gain: float32 [4096], replicated, may hold values from 0.5 to 1.5
- gate_weight: bfloat16 [4096, 14336], P(None, 'dp'), may hold values from -0.09375 to 0.09375
- up_weight: bfloat16 [4096, 14336], P(None, 'dp'), may hold values from -0.09375 to 0.09375
- down_weight: bfloat16 [14336, 4096], P('dp'), may hold values from -0.046875 to 0.046875
- batch_sizes: int32 [512], P(('rep', 'dp')), parts along dimension 0, may hold values from 1 to 2, as said below
- cache_lengths: int32 [1024], P(('rep', 'dp')), parts along dimension 0, may hold values from 1 to 512, as said below
- page_table: int32 [1024, 16], P(('rep', 'dp')), parts along dimension 0, may hold values from 0 to 31, as said below
Outputs:
- layer_output: bfloat16 [4, 1024, 4096], P(None, ('rep', 'dp')), parts along dimension 1
There are 16 independent parts, one for each index of `rep`. A program takes and returns all parts, laid end to end along the dimension named above; an argument that names none is the same for every part. Nothing has to cross between parts.
Inputs may be any that keep to these rules, and one draw needn't show every extreme that they name: `batch_sizes`: one rank has exactly 2 live sequences. `cache_lengths`: some live slot holds exactly 512 cached tokens. `page_table`: entries index the owning rank's pool; no pool page appears twice within one rank.
All inputs are finite; a program needn't handle non-finite values.
Results may differ from a plain program's by a relative error of at most 0.019.
Values may be sent and summed in bfloat16 or wider, within the bound.
A program may use at most 64 MiB of HBM per device.

v0:
```python
import jax
import jax.numpy as jnp
from jax import lax
from jax.sharding import PartitionSpec as P

D = 4096
H = 32
KVH = 4
HD = 128


neg_large = -1e30
eps = 1e-05


def local(
    layer_input,
    queries,
    new_keys,
    new_values,
    key_cache,
    value_cache,
    norm_gain,
    gate_weight,
    up_weight,
    down_weight,
    batch_sizes,
    cache_lengths,
    page_table,
):
    groups = H // KVH
    count_steps = queries.shape[0]
    slots = queries.shape[1]
    extent = page_table.shape[1] * key_cache.shape[1]
    live = jnp.arange(slots, dtype=jnp.int32) < batch_sizes[0]
    cached_keys = key_cache[page_table].reshape(slots, extent, KVH, HD)
    cached_values = value_cache[page_table].reshape(slots, extent, KVH, HD)
    query_heads = queries.reshape(count_steps, slots, KVH, groups, HD)
    fresh_keys = new_keys.reshape(count_steps, slots, KVH, HD)
    fresh_values = new_values.reshape(count_steps, slots, KVH, HD)
    scale = 1.0 / jnp.sqrt(jnp.float32(HD))
    cache_scores = (
        jnp.einsum(
            "sbkgd,blkd->sbkgl", query_heads, cached_keys, preferred_element_type=jnp.float32
        )
        * scale
    )
    fresh_scores = (
        jnp.einsum("sbkgd,tbkd->sbkgt", query_heads, fresh_keys, preferred_element_type=jnp.float32)
        * scale
    )
    cache_mask = jnp.arange(extent, dtype=jnp.int32)[None, :] < cache_lengths[:, None]
    step_ids = jnp.arange(count_steps, dtype=jnp.int32)
    fresh_mask = step_ids[None, :] <= step_ids[:, None]
    cache_scores = jnp.where(cache_mask[None, :, None, None, :], cache_scores, neg_large)
    fresh_scores = jnp.where(fresh_mask[:, None, None, None, :], fresh_scores, neg_large)
    scores = jnp.concatenate([cache_scores, fresh_scores], axis=-1)
    highest = jnp.max(scores, axis=-1, keepdims=True)
    expo = jnp.exp(scores - highest)
    weights = (expo / jnp.sum(expo, axis=-1, keepdims=True)).astype(jnp.bfloat16)
    mixed = jnp.einsum(
        "sbkgl,blkd->sbkgd",
        weights[..., :extent],
        cached_values,
        preferred_element_type=jnp.float32,
    )
    mixed = mixed + jnp.einsum(
        "sbkgt,tbkd->sbkgd", weights[..., extent:], fresh_values, preferred_element_type=jnp.float32
    )
    attention = mixed.reshape(count_steps, slots, D).astype(jnp.bfloat16)
    residual = layer_input.astype(jnp.float32) + attention.astype(jnp.float32)
    inverse = lax.rsqrt(jnp.mean(residual * residual, axis=-1, keepdims=True) + eps)
    normed = residual * inverse * norm_gain
    normed = jnp.where(live[None, :, None], normed, 0.0).astype(jnp.bfloat16)
    pieces = []
    for decode_step in range(count_steps):
        piece = lax.all_gather(normed[decode_step], "dp", axis=0, tiled=True)
        gate = jnp.dot(piece, gate_weight, preferred_element_type=jnp.float32)
        upward = jnp.dot(piece, up_weight, preferred_element_type=jnp.float32)
        hidden = (jax.nn.silu(gate) * upward).astype(jnp.bfloat16)
        pieces.append(
            lax.psum_scatter(
                jnp.dot(hidden, down_weight, preferred_element_type=jnp.float32).astype(
                    jnp.bfloat16
                ),
                "dp",
                scatter_dimension=0,
                tiled=True,
            ).astype(jnp.float32)
        )
    ffn = jnp.stack(pieces, axis=0)
    return jnp.where(live[None, :, None], residual + ffn, 0.0).astype(jnp.bfloat16)


def solution(mesh):
    placed = (
        P(None, ("rep", "dp"), None),
        P(None, ("rep", "dp"), None),
        P(None, ("rep", "dp"), None),
        P(None, ("rep", "dp"), None),
        P(("rep", "dp"), None, None),
        P(("rep", "dp"), None, None),
        P(),
        P(None, "dp"),
        P(None, "dp"),
        P("dp", None),
        P(("rep", "dp")),
        P(("rep", "dp")),
        P(("rep", "dp"), None),
    )
    return jax.shard_map(
        local, mesh=mesh, in_specs=placed, out_specs=P(None, ("rep", "dp"), None), check_vma=False
    )
```

profile of v0, /device:TPU:24, one launch (start us, length us, event | category | flops | bytes accessed | tf_op | source)
XLA Modules:
  0.0 403.6 jit_solution(6074357232184744181)
XLA Ops:
  6.6 0.8 compare_select_fusion
  7.8 0.6 gather_fusion.1
  8.9 0.5 fusion.78
  9.9 0.9 divide_convert_fusion
  10.9 1.9 gather_fusion
  13.0 1.0 convolution_bitcast_fusion.1
  14.0 1.2 fusion.10
  16.6 39.1 %all-gather = bf16[1,64,4096]{2,0,1:T(2,128)(2,1)S(1)} all-gather(bf16[1,2,4096]{2,0,1:T(2,128)(2,1)S(1)} %copy.53), channel_id=2, replica_groups=mesh['dp'=32,'rep'=16] {'dp'}, dimensions={1}, use_global_device_ids=true | all-gather | bytes 540672 | tf_op jit(solution)/shard_map/all_gather | solution.py:77
  55.8 30.0 %all-gather.1 = bf16[1,64,4096]{2,0,1:T(2,128)(2,1)S(1)} all-gather(bf16[1,2,4096]{2,0,1:T(2,128)(2,1)S(1)} %copy.54), channel_id=3, replica_groups=mesh['dp'=32,'rep'=16] {'dp'}, dimensions={1}, use_global_device_ids=true | all-gather | bytes 540672 | tf_op jit(solution)/shard_map/all_gather | solution.py:77
  85.7 3.9 fusion.28
  89.6 1.2 fusion.24
  90.9 6.2 %convolution_convert_fusion.3 = bf16[64,4096]{1,0:T(8,128)(2,1)} fusion(bf16[448,4096]{1,0:T(8,128)(2,1)} %param.22, bf16[4096,448]{0,1:T(8,128)(2,1)} %param.21, bf16[1,64,4096]{2,0,1:T(2,128)(2,1)S(1)} %all-gather, f32[64,448]{1,0:T(8,128)} %fusion.28), kind=kOutput, calls=%fused_computation.5 | convolution fusion | flops 470196224 | bytes 8503296 | tf_op jit(solution)/shard_map/dot_general | solution.py:83
  97.0 6.1 %convolution_convert_fusion.2 = bf16[64,4096]{1,0:T(8,128)(2,1)} fusion(bf16[448,4096]{1,0:T(8,128)(2,1)} %param.22, bf16[4096,448]{0,1:T(8,128)(2,1)} %param.21, bf16[1,64,4096]{2,0,1:T(2,128)(2,1)S(1)} %all-gather.1, f32[64,448]{1,0:T(8,128)S(1)} %fusion.24), kind=kOutput, calls=%fused_computation.4 | convolution fusion | flops 470196224 | bytes 8503296 | tf_op jit(solution)/shard_map/dot_general | solution.py:83
  103.2 31.5 %all-gather.2 = bf16[1,64,4096]{2,0,1:T(2,128)(2,1)S(1)} all-gather(bf16[1,2,4096]{2,0,1:T(2,128)(2,1)S(1)} %copy.55), channel_id=4, replica_groups=mesh['dp'=32,'rep'=16] {'dp'}, dimensions={1}, use_global_device_ids=true | all-gather | bytes 540672 | tf_op jit(solution)/shard_map/all_gather | solution.py:77
  134.6 3.2 fusion.20
  137.9 6.1 %convolution_convert_fusion.1 = bf16[64,4096]{1,0:T(8,128)(2,1)} fusion(bf16[448,4096]{1,0:T(8,128)(2,1)} %param.22, bf16[4096,448]{0,1:T(8,128)(2,1)} %param.21, bf16[1,64,4096]{2,0,1:T(2,128)(2,1)S(1)} %all-gather.2, f32[64,448]{1,0:T(8,128)S(1)} %fusion.20), kind=kOutput, calls=%fused_computation.3 | convolution fusion | flops 470196224 | bytes 8503296 | tf_op jit(solution)/shard_map/dot_general | solution.py:83
  144.0 30.0 %all-gather.3 = bf16[1,64,4096]{2,0,1:T(2,128)(2,1)S(1)} all-gather(bf16[1,2,4096]{2,0,1:T(2,128)(2,1)S(1)} %copy.56), channel_id=5, replica_groups=mesh['dp'=32,'rep'=16] {'dp'}, dimensions={1}, use_global_device_ids=true | all-gather | bytes 540672 | tf_op jit(solution)/shard_map/all_gather | solution.py:77
  174.0 3.2 fusion.16
  177.2 6.1 %convolution_convert_fusion = bf16[64,4096]{1,0:T(8,128)(2,1)} fusion(bf16[448,4096]{1,0:T(8,128)(2,1)} %param.22, bf16[4096,448]{0,1:T(8,128)(2,1)} %param.21, bf16[1,64,4096]{2,0,1:T(2,128)(2,1)S(1)} %all-gather.3, f32[64,448]{1,0:T(8,128)S(1)} %fusion.16), kind=kOutput, calls=%fused_computation.2 | convolution fusion | flops 470196224 | bytes 8503296 | tf_op jit(solution)/shard_map/dot_general | solution.py:83
  183.4 1.3 dynamic-slice
  185.3 208.8 %all-reduce.7.cloned.1.call-done = (bf16[64,4096]{1,0:T(8,128)(2,1)}, bf16[64,4096]{1,0:T(8,128)(2,1)}, bf16[64,4096]{1,0:T(8,128)(2,1)}, bf16[64,4096]{1,0:T(8,128)(2,1)}) async-done(((bf16[64,4096]{1,0:T(8,128)(2,1)}, bf16[64,4096]{1,0:T(8,128)(2,1)}, bf16[64,4096]{1,0:T(8,128)(2,1)}, bf16[64,4096]{1,0:T(8,128)(2,1)}), (bf16[64,4096]{1,0:T(8,128)(2,1)}, bf16[64,4096]{1,0:T(8,128)(2,1)}, ...) | async-done | bytes 2097168
  394.1 0.9 dynamic-slice_bitcast_fusion.2
  395.1 0.9 dynamic-slice_bitcast_fusion
  396.0 0.8 select_convert_fusion
  (41 shorter events, 2.3 us)
Async XLA Ops:
  6.5 1.2 copy-start
  6.5 2.2 copy-start.3
  6.5 2.2 copy-start.7
  6.5 2.3 copy-start.5
  6.5 387.6 %all-reduce.7.cloned.1.call-start = ((), (), s32[]{:S(2)}) async-start(), calls=%async_computation | async-start | bytes 4194304
  7.8 3.1 copy-start.6
  10.9 4.5 %copy-start.2 = (bf16[4,2,4096]{2,1,0:T(2,128)(2,1)S(1)}, bf16[4,2,4096]{2,1,0:T(2,128)(2,1)}, u32[]{:S(2)}) copy-start(bf16[4,2,4096]{2,1,0:T(2,128)(2,1)} %param.13) | copy-start | bytes 196612
  10.9 5.5 %copy-start.4 = (f32[4096]{0:T(1024)S(1)}, f32[4096]{0:T(1024)}, u32[]{:S(2)}) copy-start(f32[4096]{0:T(1024)} %param.19) | copy-start | bytes 49156
  15.4 74.2 %copy-start.1 = (bf16[4096,448]{0,1:T(8,128)(2,1)S(1)}, bf16[4096,448]{0,1:T(8,128)(2,1)}, u32[]{:S(2)}) copy-start(bf16[4096,448]{0,1:T(8,128)(2,1)} %param.20) | copy-start | bytes 11010052
Sparse Core Ops, SparseCore 0:
  183.5 210.5 all-reduce.6
where the time goes:
time: 406 us; the launch traced here: 404 us
  waiting for transfers between devices  209 us (51%)
  blocking collectives  130 us (32%)
  matrix products  39.1 us (10%)
  between operations  15 us (4%)
  local copies, waits for them, and re-layouts  6.91 us (2%)
    unnamed x2, waiting for transfers between devices  209 us
    all_gather x4, blocking collectives, local(): piece = lax.all_gather(normed[decode_step], 'dp', axis=0, tiled=True)  130 us
    dot_general x4, matrix products, local(): jnp.dot(hidden, down_weight, preferred_element_type=jnp.float32)  24.5 us
    dot_general x4, matrix products, local(): gate = jnp.dot(piece, gate_weight, preferred_element_type=jnp.float32)  11.6 us
  transfers between devices with their start and end apart: 1, of which 1 were waited for; matrix products, arithmetic and copies ran while one was open for 0% of the time, Pallas kernels for 0%

commit v1 on v0

v1 whole, which is shorter than its diff:
```python
import jax
import jax.numpy as jnp
from jax import lax
from jax.experimental import pallas as pl
from jax.experimental.pallas import tpu as pltpu
from jax.sharding import PartitionSpec as P

D = 4096
H = 32
KVH = 4
HD = 128
HALF = D // 2
NJ = 2
W = HALF // NJ
NC = 4
CW = HALF // NC
CHIPS = 16
POOL = 1024
KEYS = POOL + 128

masked = -1e30
eps = 1e-05
MESH = pl.DeviceIdType.MESH


def slot_of(offset):
    if offset == 8 or offset == -8:
        return 15
    return 2 * offset if offset >= 0 else -2 * offset - 1


def kernel(
    bs_ref, cl_ref, pt_ref, li_ref, q_ref, nk_ref, nv_ref, gain_ref,
    kc_ref, vc_ref, wg_ref, wu_ref, wd_ref,
    out_ref,
    li, q, nk, nv, gain, kb, vb, wgu, wd, rows, res, gath, acc, hid, own, sibs, sibr,
    sp, sm, rp, rm,
    lsem, ag_send, ag_recv, as_send, as_recv,
    ps_send, ps_recv, ms_send, ms_recv, ss_send, ss_recv,
):
    me = lax.axis_index("dp")
    core = lax.rem(me, 2)
    right = lax.rem(me + 2, 32)
    left = lax.rem(me + 30, 32)
    right2 = lax.rem(me + 4, 32)
    left2 = lax.rem(me + 28, 32)
    sib = me + 1 - 2 * core

    def remote(src, dst, send, recv, dev):
        return pltpu.make_async_remote_copy(
            src_ref=src, dst_ref=dst, send_sem=send, recv_sem=recv,
            device_id={"dp": dev}, device_id_type=MESH,
        )

    barrier = pltpu.get_barrier_semaphore()
    for dev in (left, right, left2, right2, sib):
        pl.semaphore_signal(barrier, inc=1, device_id={"dp": dev}, device_id_type=MESH)

    width = wd.shape[0]
    moves = (
        (nk_ref, nk), (nv_ref, nv), (q_ref, q),
        (kc_ref, kb.at[pl.ds(0, POOL)]), (vc_ref, vb.at[pl.ds(0, POOL)]),
        (li_ref, li), (gain_ref, gain),
        (wg_ref, wgu.at[pl.ds(0, width)]), (wu_ref, wgu.at[pl.ds(width, width)]), (wd_ref, wd),
    )
    loads = [pltpu.make_async_copy(src, dst, lsem.at[i]) for i, (src, dst) in enumerate(moves)]
    for load in loads:
        load.start()

    def stacked(ref, width):
        for s in range(4):
            rows[2 * s : 2 * s + 2, :width] = ref[s].astype(jnp.float32)
        return rows[:, :width]

    col1 = lax.broadcasted_iota(jnp.int32, (1, KEYS), 1)
    page = lax.shift_right_logical(col1, 5)
    off = jnp.bitwise_and(col1, 31)
    slot_bias = []
    for b in range(2):
        count = jnp.zeros((1, KEYS), jnp.int32)
        for i in range(16):
            count = jnp.where(page == pt_ref[b, i], cl_ref[b] - 32 * i, count)
        slot_bias.append(jnp.where(off < count, 0.0, masked))
    row8 = lax.broadcasted_iota(jnp.int32, (8, KEYS), 0)
    col8 = lax.broadcasted_iota(jnp.int32, (8, KEYS), 1) - POOL
    rowb = jnp.bitwise_and(row8, 1)
    bias = jnp.where(
        rowb == 0,
        jnp.broadcast_to(slot_bias[0], (8, KEYS)),
        jnp.broadcast_to(slot_bias[1], (8, KEYS)),
    )
    fresh = (
        (col8 >= 0)
        & (col8 < 8)
        & (jnp.bitwise_and(col8, 1) == rowb)
        & (lax.shift_right_arithmetic(col8, 1) <= lax.shift_right_logical(row8, 1))
    )
    bias = jnp.where(fresh, 0.0, bias)

    for load in loads[:2]:
        load.wait()
    zeros8 = jnp.zeros((8, KVH * HD), jnp.float32)
    kb[pl.ds(POOL, 16)] = jnp.concatenate([stacked(nk, KVH * HD), zeros8], 0).astype(jnp.bfloat16)
    vb[pl.ds(POOL, 16)] = jnp.concatenate([stacked(nv, KVH * HD), zeros8], 0).astype(jnp.bfloat16)
    kb[pl.ds(POOL + 16, 112)] = jnp.zeros((112, KVH * HD), jnp.bfloat16)
    vb[pl.ds(POOL + 16, 112)] = jnp.zeros((112, KVH * HD), jnp.bfloat16)
    loads[2].wait()
    qf = stacked(q, D)
    scale = 1.0 / jnp.sqrt(jnp.float32(HD))
    loads[3].wait()
    heads = []
    for k in range(KVH):
        qk = jnp.concatenate(
            [qf[:, (8 * k + g) * HD : (8 * k + g + 1) * HD] for g in range(8)], 0
        ).astype(jnp.bfloat16)
        scores = lax.dot_general(
            qk, kb[:, k * HD : (k + 1) * HD], (((1,), (1,)), ((), ())),
            preferred_element_type=jnp.float32,
        )
        scores = (scores.reshape(8, 8, KEYS) * scale + bias[None]).reshape(64, KEYS)
        highest = jnp.max(scores, axis=-1, keepdims=True)
        expo = jnp.exp(scores - highest)
        total = jnp.sum(expo, axis=-1, keepdims=True)
        if k == 0:
            loads[4].wait()
        mixed = jnp.dot(
            expo.astype(jnp.bfloat16), vb[:, k * HD : (k + 1) * HD],
            preferred_element_type=jnp.float32,
        ) / total
        heads += [mixed[8 * g : 8 * g + 8] for g in range(8)]
    attention = jnp.concatenate(heads, 1).astype(jnp.bfloat16).astype(jnp.float32)
    loads[5].wait()
    residual = stacked(li, D) + attention
    res[...] = residual
    inverse = lax.rsqrt(jnp.mean(residual * residual, axis=-1, keepdims=True) + eps)
    loads[6].wait()
    normed = residual * inverse * gain[...]
    live = jnp.bitwise_and(lax.broadcasted_iota(jnp.int32, (8, D), 0), 1) < bs_ref[0]
    normed = jnp.where(live, normed, 0.0)
    for c in range(NC):
        both = [normed[:, (2 * c + fold) * CW : (2 * c + fold + 1) * CW] for fold in range(2)]
        gath[0, 0, :, c * CW : (c + 1) * CW] = jnp.concatenate(both, 0).astype(jnp.bfloat16)
    acc[...] = jnp.zeros_like(acc)

    pl.semaphore_wait(barrier, 5)

    def lanes(j):
        return pl.ds(j * W, W)

    def ag(src, dst, j, dev):
        return remote(
            gath.at[0, src, :, lanes(j)], gath.at[0, dst, :, lanes(j)],
            ag_send.at[0], ag_recv.at[dst, j], dev,
        )

    groups = ((0, 1), (1, 4), (5, 4), (9, 4), (13, 3))

    def ag_sib(group):
        part = pl.ds(*groups[group])
        return remote(gath.at[0, part], gath.at[1, part], as_send.at[0], as_recv.at[group], sib)

    def spread(distance, j):
        for sign, one, two in ((-1, right, right2), (1, left, left2)):
            source = slot_of(sign * distance)
            if distance < 6 or (j < NJ // 2) == (sign < 0):
                ag(source, slot_of(sign * (distance + 2)), j, two).start()
            ag(source, slot_of(sign * (distance + 1)), j, one).start()

    def arrive(distance, j):
        for sign, dev in ((-1, right), (1, left)):
            if distance < 8 or (j < NJ // 2) == (sign < 0):
                ag(0, slot_of(sign * distance), j, dev).wait_recv()

    for j in range(NJ):
        spread(0, j)
    ag_sib(0).start()

    def piece(c):
        return pl.ds(c * CW, CW)

    def features(c):
        return pl.ds(c * 2 * CW, 2 * CW)

    def gate_up(half, c):
        block = gath[:, pl.ds(half * 8, 8), :, piece(c)].astype(jnp.float32)
        block = block.reshape(16, 2, 8, CW)
        block = jnp.concatenate([block[:, fold].reshape(128, CW) for fold in range(2)], 1)
        acc[half] += lax.dot_general(
            wgu[:, features(c)], block.astype(jnp.bfloat16), (((1,), (1,)), ((), ())),
            preferred_element_type=jnp.float32,
        )

    def activate(half):
        gate = acc[half, :width]
        value = gate / (1.0 + jnp.exp(-gate)) * acc[half, width:]
        hid[half] = value.T.astype(jnp.bfloat16)

    for stage in range(1, 4):
        for j in range(NJ):
            arrive(2 * stage, j)
            spread(2 * stage, j)
        for j in range(NJ):
            arrive(2 * stage - 1, j)
        ag_sib(stage).start()
    for group in range(3):
        ag_sib(group).wait_recv()
    loads[7].wait()
    loads[8].wait()

    def near(c, carry):
        gate_up(0, c)
        return carry

    lax.fori_loop(0, NC, near, 0)
    activate(0)
    for j in range(NJ):
        arrive(7, j)
        arrive(8, j)
    ag_sib(4).start()
    for group in range(3, 5):
        ag_sib(group).wait_recv()

    def far(c, carry):
        gate_up(1, c)
        return carry

    lax.fori_loop(0, NC, far, 0)
    activate(1)

    loads[9].wait()

    def sib_sum(half, c):
        slots = pl.ds(half * 8, 8)
        return remote(
            sibs.at[slots, :, piece(c)], sibr.at[slots, :, piece(c)],
            ss_send.at[0], ss_recv.at[half, c], sib,
        )

    def down(half, c):
        term = jnp.dot(hid[half], wd[:, features(c)], preferred_element_type=jnp.float32)
        both = [term[:, fold * CW : (fold + 1) * CW].reshape(2, 8, 1, 8, CW) for fold in range(2)]
        both = jnp.concatenate(both, 2).reshape(2, 8, 16, CW)
        sibs[pl.ds(half * 8, 8), :, piece(c)] = both[1].astype(jnp.bfloat16)
        sib_sum(half, c).start()
        own[pl.ds(half * 8, 8), :, piece(c)] = both[0]

    def down_far(c, carry):
        down(1, c)
        return carry

    lax.fori_loop(0, NC, down_far, 0)

    def plus(m, j):
        return remote(
            sp.at[m - 1, :, lanes(j)], rp.at[m - 1, :, lanes(j)],
            ps_send.at[m // 8], ps_recv.at[m - 1, j], right if m % 2 else right2,
        )

    def minus(m, j):
        return remote(
            sm.at[m - 1, :, lanes(j)], rm.at[m - 1, :, lanes(j)],
            ms_send.at[m // 8], ms_recv.at[m - 1, j], left if m % 2 else left2,
        )

    sides = ((1, plus, sp, rp), (-1, minus, sm, rm))

    def pass_on(m, j, arrivals):
        for sign, copy, leaving, arrived in sides:
            if m == 8 and (j < NJ // 2) != (sign > 0):
                continue
            slot = slot_of(sign * m)
            value = own[slot, :, lanes(j)] + sibr[slot, :, lanes(j)].astype(jnp.float32)
            for source in arrivals:
                if source == 8 and (j < NJ // 2) != (sign > 0):
                    continue
                copy(source, j).wait_recv()
                value = value + arrived[source - 1, :, lanes(j)].astype(jnp.float32)
            leaving[m - 1, :, lanes(j)] = value.astype(jnp.bfloat16)
            copy(m, j).start()

    for j in range(NJ):
        for c in range(j * NC // NJ, (j + 1) * NC // NJ):
            sib_sum(1, c).wait_recv()
        pass_on(8, j, ())
        pass_on(7, j, ())
    for j in range(NJ):
        pass_on(5, j, ())
    down(0, 0)
    down(0, 1)
    for j in range(NJ):
        pass_on(6, j, (7, 8))
    down(0, 2)
    down(0, 3)
    for c in range(NC):
        sib_sum(0, c).wait_recv()
    for j in range(NJ):
        pass_on(3, j, ())
    for j in range(NJ):
        pass_on(4, j, (5, 6))
    for j in range(NJ):
        pass_on(1, j, ())
    for j in range(NJ):
        pass_on(2, j, (3, 4))

    alive = jnp.bitwise_and(lax.broadcasted_iota(jnp.int32, (8, CW), 0), 1) < bs_ref[0]
    for j in range(NJ):
        for m in (1, 2):
            plus(m, j).wait_recv()
            minus(m, j).wait_recv()
        for c in range(j * NC // NJ, (j + 1) * NC // NJ):
            value = own[0, :, piece(c)] + sibr[0, :, piece(c)].astype(jnp.float32)
            for m in (1, 2):
                for arrived in (rp, rm):
                    value = value + arrived[m - 1, :, piece(c)].astype(jnp.float32)
            for fold in range(2):
                place = pl.ds((2 * c + fold) * CW, CW)
                done = res[:, place] + value[8 * fold : 8 * fold + 8]
                out_ref[:, place] = jnp.where(alive, done, 0.0).astype(jnp.bfloat16)

    def sent(part, sem):
        remote(part, part, sem, sem, sib).wait_send()

    sent(gath.at[0, pl.ds(1, 15)], ag_send.at[0])
    sent(gath.at[0], as_send.at[0])
    sent(sibs, ss_send.at[0])
    sent(sp.at[7, :, pl.ds(0, HALF // 2)], ps_send.at[1])
    sent(sm.at[7, :, pl.ds(0, HALF // 2)], ms_send.at[1])
    sent(sp.at[pl.ds(0, 7)], ps_send.at[0])
    sent(sm.at[pl.ds(0, 7)], ms_send.at[0])


def local(
    layer_input, queries, new_keys, new_values, key_cache, value_cache, norm_gain,
    gate_weight, up_weight, down_weight, batch_sizes, cache_lengths, page_table,
):
    vmem = pl.BlockSpec(memory_space=pltpu.VMEM)
    smem = pl.BlockSpec(memory_space=pltpu.SMEM)
    hbm = pl.BlockSpec(memory_space=pltpu.HBM)
    width = down_weight.shape[0]
    bf16, f32 = jnp.bfloat16, jnp.float32
    dma = pltpu.SemaphoreType.DMA
    out = pl.pallas_call(
        kernel,
        out_shape=jax.ShapeDtypeStruct((8, D), bf16),
        in_specs=[smem] * 3 + [hbm] * 10,
        out_specs=vmem,
        scratch_shapes=[
            pltpu.VMEM((4, 2, D), bf16),
            pltpu.VMEM((4, 2, D), bf16),
            pltpu.VMEM((4, 2, KVH * HD), bf16),
            pltpu.VMEM((4, 2, KVH * HD), bf16),
            pltpu.VMEM((1, D), f32),
            pltpu.VMEM((KEYS, KVH * HD), bf16),
            pltpu.VMEM((KEYS, KVH * HD), bf16),
            pltpu.VMEM((2 * width, D), bf16),
            pltpu.VMEM((width, D), bf16),
            pltpu.VMEM((8, D), f32),
            pltpu.VMEM((8, D), f32),
            pltpu.VMEM((2, 16, 16, HALF), bf16),
            pltpu.VMEM((2, 2 * width, 128), f32),
            pltpu.VMEM((2, 128, width), bf16),
            pltpu.VMEM((16, 16, HALF), f32),
            pltpu.VMEM((16, 16, HALF), bf16),
            pltpu.VMEM((16, 16, HALF), bf16),
            pltpu.VMEM((8, 16, HALF), bf16),
            pltpu.VMEM((8, 16, HALF), bf16),
            pltpu.VMEM((8, 16, HALF), bf16),
            pltpu.VMEM((8, 16, HALF), bf16),
            dma((10,)),
            dma((1,)),
            dma((16, NJ)),
            dma((1,)),
            dma((5,)),
            dma((2,)),
            dma((8, NJ)),
            dma((2,)),
            dma((8, NJ)),
            dma((1,)),
            dma((2, NC)),
        ],
        compiler_params=pltpu.CompilerParams(
            collective_id=0, has_side_effects=True, vmem_limit_bytes=56 * 1024 * 1024
        ),
    )(
        batch_sizes,
        cache_lengths,
        page_table,
        layer_input,
        queries,
        new_keys,
        new_values,
        norm_gain.reshape(1, D),
        key_cache.reshape(POOL, KVH * HD),
        value_cache.reshape(POOL, KVH * HD),
        gate_weight.T,
        up_weight.T,
        down_weight,
    )
    return out.reshape(4, 2, D)


def solution(mesh):
    placed = (
        P(None, ("rep", "dp"), None),
        P(None, ("rep", "dp"), None),
        P(None, ("rep", "dp"), None),
        P(None, ("rep", "dp"), None),
        P(("rep", "dp"), None, None),
        P(("rep", "dp"), None, None),
        P(),
        P(None, "dp"),
        P(None, "dp"),
        P("dp", None),
        P(("rep", "dp")),
        P(("rep", "dp")),
        P(("rep", "dp"), None),
    )
    return jax.shard_map(
        local, mesh=mesh, in_specs=placed, out_specs=P(None, ("rep", "dp"), None), check_vma=False
    )
```

time: 406 us -> 61.9 us (0.15)
  waiting for transfers between devices: 209 us -> 0 us
  blocking collectives: 130 us -> 0 us
  Pallas kernels: 0 us -> 59.2 us
  matrix products: 39.1 us -> 0 us
  between operations: 15 us -> 0.66 us
  local copies, waits for them, and re-layouts: 6.91 us -> 1.52 us
    unnamed x2 -> x0, waiting for transfers between devices: 209 us -> none
    all_gather x4 -> x0, blocking collectives: 130 us -> none  [local(): piece = lax.all_gather(normed[decode_step], 'dp', axis=0, tiled=True)]
    pallas_call x0 -> x1, Pallas kernels: none -> 59.2 us  [local(): pl.pallas_call(kernel, out_shape=jax.ShapeDtypeStruct((8, D), bf16), in_s...]
    dot_general x12 -> x0, matrix products: 39.1 us -> none  [the longest x4 24.5 us: local(): jnp.dot(hidden, down_weight, preferred_element_type=jnp.float32)]
  transfers between devices with their start and end apart: 1 -> 0, of which waited for: 1 -> 0; matrix products, arithmetic and copies ran while one was open for 0% -> 0% of each run, Pallas kernels for 0% -> 0%
where the time goes in v1:
time: 61.9 us; the launch traced here: 61.4 us
  Pallas kernels  59.2 us (96%)
  local copies, waits for them, and re-layouts  1.52 us (2%)
  between operations  0.66 us (1%)
    pallas_call x1, Pallas kernels, local(): pl.pallas_call(kernel, out_shape=jax.ShapeDtypeStruct((8, D), bf16), in_s...  59.2 us
    reshape x1, local copies, waits for them, and re-layouts, local(): return out.reshape(4, 2, D)  1.52 us

profile of v1, /device:TPU:24, one launch (start us, length us, event | category | flops | bytes accessed | tf_op | source)
XLA Modules:
  0.0 61.4 jit_solution(3269857912332536577)
XLA Ops:
  0.7 59.2 %shard_map.127 = bf16[8,4096]{1,0:T(8,128)(2,1)} custom-call(s32[1]{0:T(128)S(6)} %copy.14.bs_ref, s32[2]{0:T(128)} %cl_ref.1, s32[2,16]{1,0:T(2,128)} %pt_ref.1, bf16[4,2,4096]{2,1,0:T(2,128)(2,1)} %li_ref.1, bf16[4,2,4096]{2,1,0:T(2,128)(2,1)} %q_ref.1, bf16[4,2,512]{2,1,0:T(2,128)(2,1)} %nk_ref.1, bf16[4,2,512]{2,1,0:T(2,128)(2,1)} %nv_ref.1, ...), custom_call_target="tpu_custom_call" | custom-call | tf_op jit(solution)/shard_map/pallas_call | solution.py:342
  59.9 1.5 %reshape.15 = bf16[4,2,4096]{2,1,0:T(2,128)(2,1)} reshape(bf16[8,4096]{1,0:T(8,128)(2,1)} %shard_map.127) | data formatting | bytes 131072 | tf_op jit(solution)/shard_map/reshape | solution.py:399

commit v2 on v1

v2 whole, which is shorter than its diff:
```python
import jax
import jax.numpy as jnp
from jax import lax
from jax.experimental import pallas as pl
from jax.experimental.pallas import tpu as pltpu
from jax.sharding import PartitionSpec as P

D = 4096
H = 32
KVH = 4
HD = 128
HALF = D // 2
NJ = 2
W = HALF // NJ
NC = 4
CW = HALF // NC
CHIPS = 16
POOL = 1024
KEYS = POOL + 128

PARENT = {1: 0, 2: 0, 3: 2, 4: 2, 5: 4, 6: 4, 7: 6, 8: 6}


def children(m):
    return [n for n in sorted(PARENT, reverse=True) if PARENT[n] == m]


masked = -1e30
eps = 1e-05
MESH = pl.DeviceIdType.MESH


def slot_of(offset):
    if offset == 8 or offset == -8:
        return 15
    return 2 * offset if offset >= 0 else -2 * offset - 1


def kernel(
    bs_in, cl_in, pt_in, li_ref, q_ref, nk_ref, nv_ref, gain_ref,
    kc_ref, vc_ref, wg_ref, wu_ref, wd_ref,
    out_ref,
    bs, cl, pt, li, q, nk, nv, gain, kb, vb, wgu, wd, rows, res, gath, acc, hid, own, sibs, sibr,
    sp, sm, rp, rm,
    lsem, ag_send, ag_recv, as_send, as_recv,
    ps_send, ps_recv, ms_send, ms_recv, ss_send, ss_recv,
):
    me = lax.axis_index("dp")
    core = lax.rem(me, 2)
    steps = sorted({n - m for n, m in PARENT.items()})
    right = {step: lax.rem(me + 2 * step, 32) for step in steps}
    left = {step: lax.rem(me + 32 - 2 * step, 32) for step in steps}
    sib = me + 1 - 2 * core

    def remote(src, dst, send, recv, dev):
        return pltpu.make_async_remote_copy(
            src_ref=src, dst_ref=dst, send_sem=send, recv_sem=recv,
            device_id={"dp": dev}, device_id_type=MESH,
        )

    barrier = pltpu.get_barrier_semaphore()
    partners = [*left.values(), *right.values(), sib]
    for dev in partners:
        pl.semaphore_signal(barrier, inc=1, device_id={"dp": dev}, device_id_type=MESH)

    width = wd.shape[0]
    moves = (
        (bs_in, bs), (cl_in, cl), (pt_in, pt),
        (nk_ref, nk), (nv_ref, nv), (q_ref, q),
        (kc_ref, kb.at[pl.ds(0, POOL)]), (vc_ref, vb.at[pl.ds(0, POOL)]),
        (li_ref, li), (gain_ref, gain),
        (wg_ref, wgu.at[pl.ds(0, width)]), (wu_ref, wgu.at[pl.ds(width, width)]), (wd_ref, wd),
    )
    loads = [pltpu.make_async_copy(src, dst, lsem.at[i]) for i, (src, dst) in enumerate(moves)]
    for load in loads[:10]:
        load.start()

    def stacked(ref, width):
        for s in range(4):
            rows[2 * s : 2 * s + 2, :width] = ref[s].astype(jnp.float32)
        return rows[:, :width]

    for load in loads[:3]:
        load.wait()
    col1 = lax.broadcasted_iota(jnp.int32, (1, KEYS), 1)
    page = lax.shift_right_logical(col1, 5)
    off = jnp.bitwise_and(col1, 31)
    slot_bias = []
    for b in range(2):
        count = jnp.zeros((1, KEYS), jnp.int32)
        for i in range(16):
            count = jnp.where(page == pt[b, i], cl[b] - 32 * i, count)
        slot_bias.append(jnp.where(off < count, 0.0, masked))
    row8 = lax.broadcasted_iota(jnp.int32, (8, KEYS), 0)
    col8 = lax.broadcasted_iota(jnp.int32, (8, KEYS), 1) - POOL
    rowb = jnp.bitwise_and(row8, 1)
    bias = jnp.where(
        rowb == 0,
        jnp.broadcast_to(slot_bias[0], (8, KEYS)),
        jnp.broadcast_to(slot_bias[1], (8, KEYS)),
    )
    fresh = (
        (col8 >= 0)
        & (col8 < 8)
        & (jnp.bitwise_and(col8, 1) == rowb)
        & (lax.shift_right_arithmetic(col8, 1) <= lax.shift_right_logical(row8, 1))
    )
    bias = jnp.where(fresh, 0.0, bias)

    for load in loads[3:5]:
        load.wait()
    zeros8 = jnp.zeros((8, KVH * HD), jnp.float32)
    kb[pl.ds(POOL, 16)] = jnp.concatenate([stacked(nk, KVH * HD), zeros8], 0).astype(jnp.bfloat16)
    vb[pl.ds(POOL, 16)] = jnp.concatenate([stacked(nv, KVH * HD), zeros8], 0).astype(jnp.bfloat16)
    kb[pl.ds(POOL + 16, 112)] = jnp.zeros((112, KVH * HD), jnp.bfloat16)
    vb[pl.ds(POOL + 16, 112)] = jnp.zeros((112, KVH * HD), jnp.bfloat16)
    loads[5].wait()
    qf = stacked(q, D)
    scale = 1.0 / jnp.sqrt(jnp.float32(HD))
    loads[6].wait()
    heads = []
    blank = jnp.zeros((64, HD), jnp.float32)
    for pair in range(KVH // 2):
        both = [
            jnp.concatenate(
                [qf[:, (16 * pair + 8 * i + g) * HD : (16 * pair + 8 * i + g + 1) * HD] for g in range(8)], 0
            )
            for i in range(2)
        ]
        both = jnp.concatenate(
            [jnp.concatenate([both[0], blank], 1), jnp.concatenate([blank, both[1]], 1)], 0
        ).astype(jnp.bfloat16)
        place = slice(2 * pair * HD, 2 * (pair + 1) * HD)
        scores = lax.dot_general(
            both, kb[:, place], (((1,), (1,)), ((), ())), preferred_element_type=jnp.float32
        )
        scores = (scores.reshape(16, 8, KEYS) * scale + bias[None]).reshape(128, KEYS)
        highest = jnp.max(scores, axis=-1, keepdims=True)
        expo = jnp.exp(scores - highest)
        total = jnp.sum(expo, axis=-1, keepdims=True)
        if pair == 0:
            loads[7].wait()
            for load in loads[10:]:
                load.start()
        mixed = jnp.dot(
            expo.astype(jnp.bfloat16), vb[:, place], preferred_element_type=jnp.float32
        ) / total
        for i in range(2):
            heads += [
                mixed[64 * i + 8 * g : 64 * i + 8 * g + 8, i * HD : (i + 1) * HD] for g in range(8)
            ]
    attention = jnp.concatenate(heads, 1).astype(jnp.bfloat16).astype(jnp.float32)
    loads[8].wait()
    residual = stacked(li, D) + attention
    res[...] = residual
    inverse = lax.rsqrt(jnp.mean(residual * residual, axis=-1, keepdims=True) + eps)
    loads[9].wait()
    normed = residual * inverse * gain[...]
    live = jnp.bitwise_and(lax.broadcasted_iota(jnp.int32, (8, D), 0), 1) < bs[0]
    normed = jnp.where(live, normed, 0.0)
    for c in range(NC):
        both = [normed[:, (2 * c + fold) * CW : (2 * c + fold + 1) * CW] for fold in range(2)]
        gath[0, 0, :, c * CW : (c + 1) * CW] = jnp.concatenate(both, 0).astype(jnp.bfloat16)
    pl.semaphore_wait(barrier, len(partners))

    def lanes(j):
        return pl.ds(j * W, W)

    def ag(src, dst, j, dev):
        return remote(
            gath.at[0, src, :, lanes(j)], gath.at[0, dst, :, lanes(j)],
            ag_send.at[0], ag_recv.at[dst, j], dev,
        )

    groups = ((0, 1), (1, 4), (5, 4), (9, 4), (13, 3))

    def ag_sib(group, j):
        part = pl.ds(*groups[group])
        return remote(
            gath.at[0, part, :, lanes(j)], gath.at[1, part, :, lanes(j)],
            as_send.at[0], as_recv.at[group, j], sib,
        )

    def goes(m, j, sign):
        return m < 8 or (j < NJ // 2) == (sign > 0)

    def spread(m, j):
        for n in children(m):
            for sign, devices in ((1, right), (-1, left)):
                if goes(n, j, sign):
                    ag(slot_of(-sign * m), slot_of(-sign * n), j, devices[n - m]).start()

    def arrive(m, j):
        for sign in (1, -1):
            if goes(m, j, sign):
                ag(0, slot_of(-sign * m), j, right[1]).wait_recv()

    for j in range(NJ):
        spread(0, j)
    for j in range(NJ):
        ag_sib(0, j).start()

    def piece(c):
        return pl.ds(c * CW, CW)

    def features(c):
        return pl.ds(c * 2 * CW, 2 * CW)

    def gate_up(half, j):
        block = gath[:, pl.ds(half * 8, 8), :, lanes(j)].astype(jnp.float32)
        block = block.reshape(16, 2, 8, W)
        block = jnp.concatenate(
            [
                block[:, fold, :, c * CW : (c + 1) * CW].reshape(128, CW)
                for c in range(NC // NJ)
                for fold in range(2)
            ],
            1,
        )
        term = lax.dot_general(
            wgu[:, pl.ds(j * 2 * W, 2 * W)], block.astype(jnp.bfloat16),
            (((1,), (1,)), ((), ())), preferred_element_type=jnp.float32,
        )
        if j == 0:
            acc[half] = term
        else:
            acc[half] += term

    def activate(half):
        gate = acc[half, :width]
        value = gate / (1.0 + jnp.exp(-gate)) * acc[half, width:]
        hid[half] = value.T.astype(jnp.bfloat16)

    def sib_sum(half, c):
        slots = pl.ds(half * 8, 8)
        return remote(
            sibs.at[slots, :, piece(c)], sibr.at[slots, :, piece(c)],
            ss_send.at[0], ss_recv.at[half, c], sib,
        )

    def down(half):
        def step(c, carry):
            term = jnp.dot(hid[half], wd[:, features(c)], preferred_element_type=jnp.float32)
            both = [
                term[:, fold * CW : (fold + 1) * CW].reshape(2, 8, 1, 8, CW) for fold in range(2)
            ]
            both = jnp.concatenate(both, 2).reshape(2, 8, 16, CW)
            slots = pl.ds(half * 8, 8)
            sibs[slots, :, piece(c)] = both[1].astype(jnp.bfloat16)
            sib_sum(half, c).start()
            own[slots, :, piece(c)] = both[0]
            return carry

        lax.fori_loop(0, NC, step, 0)

    def plus(m, j):
        return remote(
            sp.at[m - 1, :, lanes(j)], rp.at[m - 1, :, lanes(j)],
            ps_send.at[m // 8], ps_recv.at[m - 1, j], right[m - PARENT[m]],
        )

    def minus(m, j):
        return remote(
            sm.at[m - 1, :, lanes(j)], rm.at[m - 1, :, lanes(j)],
            ms_send.at[m // 8], ms_recv.at[m - 1, j], left[m - PARENT[m]],
        )

    sides = ((1, plus, sp, rp), (-1, minus, sm, rm))

    def pass_on(m, j):
        for sign, copy, leaving, arrived in sides:
            if not goes(m, j, sign):
                continue
            slot = slot_of(sign * m)
            value = own[slot, :, lanes(j)] + sibr[slot, :, lanes(j)].astype(jnp.float32)
            for source in children(m):
                if goes(source, j, sign):
                    copy(source, j).wait_recv()
                    value = value + arrived[source - 1, :, lanes(j)].astype(jnp.float32)
            leaving[m - 1, :, lanes(j)] = value.astype(jnp.bfloat16)
            copy(m, j).start()

    def gathered(group):
        for j in range(NJ):
            ag_sib(group, j).wait_recv()

    for stage in range(1, 4):
        for j in range(NJ):
            arrive(2 * stage, j)
            spread(2 * stage, j)
        for j in range(NJ):
            arrive(2 * stage - 1, j)
            ag_sib(stage, j).start()

    for group in range(3):
        gathered(group)
    loads[10].wait()
    loads[11].wait()
    for j in range(NJ):
        gate_up(0, j)
    activate(0)
    loads[12].wait()
    down(0)

    for j in range(NJ):
        arrive(7, j)
        arrive(8, j)
        ag_sib(4, j).start()
    for c in range(NC):
        sib_sum(0, c).wait_recv()
    for j in range(NJ):
        pass_on(3, j)

    for j in range(NJ):
        for group in (3, 4):
            ag_sib(group, j).wait_recv()
        gate_up(1, j)
    activate(1)
    down(1)
    for j in range(NJ):
        pass_on(1, j)
    for j in range(NJ):
        for c in range(j * NC // NJ, (j + 1) * NC // NJ):
            sib_sum(1, c).wait_recv()
        for m in (8, 7):
            pass_on(m, j)
    for m in (5, 6, 4, 2):
        for j in range(NJ):
            pass_on(m, j)

    alive = jnp.bitwise_and(lax.broadcasted_iota(jnp.int32, (8, CW), 0), 1) < bs[0]
    for j in range(NJ):
        for m in children(0):
            plus(m, j).wait_recv()
            minus(m, j).wait_recv()
        for c in range(j * NC // NJ, (j + 1) * NC // NJ):
            value = own[0, :, piece(c)] + sibr[0, :, piece(c)].astype(jnp.float32)
            for m in children(0):
                for arrived in (rp, rm):
                    value = value + arrived[m - 1, :, piece(c)].astype(jnp.float32)
            for fold in range(2):
                place = pl.ds((2 * c + fold) * CW, CW)
                done = res[:, place] + value[8 * fold : 8 * fold + 8]
                out_ref[:, place] = jnp.where(alive, done, 0.0).astype(jnp.bfloat16)

    def sent(part, sem):
        remote(part, part, sem, sem, sib).wait_send()

    sent(gath.at[0, pl.ds(1, 15)], ag_send.at[0])
    sent(gath.at[0], as_send.at[0])
    sent(sibs, ss_send.at[0])
    sent(sp.at[7, :, pl.ds(0, HALF // 2)], ps_send.at[1])
    sent(sm.at[7, :, pl.ds(0, HALF // 2)], ms_send.at[1])
    sent(sp.at[pl.ds(0, 7)], ps_send.at[0])
    sent(sm.at[pl.ds(0, 7)], ms_send.at[0])


def local(
    layer_input, queries, new_keys, new_values, key_cache, value_cache, norm_gain,
    gate_weight, up_weight, down_weight, batch_sizes, cache_lengths, page_table,
):
    vmem = pl.BlockSpec(memory_space=pltpu.VMEM)
    hbm = pl.BlockSpec(memory_space=pltpu.HBM)
    width = down_weight.shape[0]
    bf16, f32 = jnp.bfloat16, jnp.float32
    dma = pltpu.SemaphoreType.DMA
    out = pl.pallas_call(
        kernel,
        out_shape=pltpu.VMEM((8, D), bf16),
        in_specs=[hbm] * 13,
        out_specs=vmem,
        scratch_shapes=[
            pltpu.SMEM((1,), jnp.int32),
            pltpu.SMEM((2,), jnp.int32),
            pltpu.SMEM((2, 16), jnp.int32),
            pltpu.VMEM((4, 2, D), bf16),
            pltpu.VMEM((4, 2, D), bf16),
            pltpu.VMEM((4, 2, KVH * HD), bf16),
            pltpu.VMEM((4, 2, KVH * HD), bf16),
            pltpu.VMEM((1, D), f32),
            pltpu.VMEM((KEYS, KVH * HD), bf16),
            pltpu.VMEM((KEYS, KVH * HD), bf16),
            pltpu.VMEM((2 * width, D), bf16),
            pltpu.VMEM((width, D), bf16),
            pltpu.VMEM((8, D), f32),
            pltpu.VMEM((8, D), f32),
            pltpu.VMEM((2, 16, 16, HALF), bf16),
            pltpu.VMEM((2, 2 * width, 128), f32),
            pltpu.VMEM((2, 128, width), bf16),
            pltpu.VMEM((16, 16, HALF), f32),
            pltpu.VMEM((16, 16, HALF), bf16),
            pltpu.VMEM((16, 16, HALF), bf16),
            pltpu.VMEM((8, 16, HALF), bf16),
            pltpu.VMEM((8, 16, HALF), bf16),
            pltpu.VMEM((8, 16, HALF), bf16),
            pltpu.VMEM((8, 16, HALF), bf16),
            dma((13,)),
            dma((1,)),
            dma((16, NJ)),
            dma((1,)),
            dma((5, NJ)),
            dma((2,)),
            dma((8, NJ)),
            dma((2,)),
            dma((8, NJ)),
            dma((1,)),
            dma((2, NC)),
        ],
        compiler_params=pltpu.CompilerParams(
            collective_id=0, has_side_effects=True, vmem_limit_bytes=56 * 1024 * 1024
        ),
    )(
        batch_sizes,
        cache_lengths,
        page_table,
        layer_input,
        queries,
        new_keys,
        new_values,
        norm_gain.reshape(1, D),
        key_cache.reshape(POOL, KVH * HD),
        value_cache.reshape(POOL, KVH * HD),
        gate_weight.T,
        up_weight.T,
        down_weight,
    )
    return out.reshape(4, 2, D)


def solution(mesh):
    placed = (
        P(None, ("rep", "dp"), None),
        P(None, ("rep", "dp"), None),
        P(None, ("rep", "dp"), None),
        P(None, ("rep", "dp"), None),
        P(("rep", "dp"), None, None),
        P(("rep", "dp"), None, None),
        P(),
        P(None, "dp"),
        P(None, "dp"),
        P("dp", None),
        P(("rep", "dp")),
        P(("rep", "dp")),
        P(("rep", "dp"), None),
    )
    return jax.shard_map(
        local, mesh=mesh, in_specs=placed, out_specs=P(None, ("rep", "dp"), None), check_vma=False
    )
```

time: 61.9 us -> 60.6 us (0.979)
  local copies, waits for them, and re-layouts: 1.52 us -> 0.69 us
    reshape x1, local copies, waits for them, and re-layouts: 1.52 us -> 0.69 us  [local(): return out.reshape(4, 2, D)]
where the time goes in v2:
time: 60.6 us; the launch traced here: 60.4 us
  Pallas kernels  59.1 us (98%)
  local copies, waits for them, and re-layouts  0.69 us (1%)
  between operations  0.66 us (1%)
    pallas_call x1, Pallas kernels, local(): pl.pallas_call(kernel, out_shape=pltpu.VMEM((8, D), bf16), in_specs=[hbm]...  59.1 us

profile of v2, /device:TPU:24, one launch (start us, length us, event | category | flops | bytes accessed | tf_op | source)
XLA Modules:
  0.0 60.4 jit_solution(11338894116300936111)
XLA Ops:
  0.7 59.1 %shard_map.127 = bf16[8,4096]{1,0:T(8,128)(2,1)S(1)} custom-call(s32[1]{0:T(128)S(6)} %copy.14.bs_in, s32[2]{0:T(128)} %cl_in.1, s32[2,16]{1,0:T(2,128)} %pt_in.1, bf16[4,2,4096]{2,1,0:T(2,128)(2,1)} %li_ref.1, bf16[4,2,4096]{2,1,0:T(2,128)(2,1)} %q_ref.1, bf16[4,2,512]{2,1,0:T(2,128)(2,1)} %nk_ref.1, bf16[4,2,512]{2,1,0:T(2,128)(2,1)} %nv_ref.1, ...), custom_call_target="tpu_custom_call" | custom-call | tf_op jit(solution)/shard_map/pallas_call | solution.py:367
  59.7 0.7 %reshape.15 = bf16[4,2,4096]{2,1,0:T(2,128)(2,1)} reshape(bf16[8,4096]{1,0:T(8,128)(2,1)S(1)} %shard_map.127) | data formatting | bytes 131072 | tf_op jit(solution)/shard_map/reshape | solution.py:427

commit v3 on v2

--- a/solution.py
+++ b/solution.py
@@ -12,6 +12,7 @@
 HALF = D // 2
 NJ = 2
 W = HALF // NJ
+SCALE = 128
 NC = 4
 CW = HALF // NC
 CHIPS = 16
@@ -64,24 +65,73 @@
         pl.semaphore_signal(barrier, inc=1, device_id={"dp": dev}, device_id_type=MESH)
 
     width = wd.shape[0]
-    moves = (
-        (bs_in, bs), (cl_in, cl), (pt_in, pt),
-        (nk_ref, nk), (nv_ref, nv), (q_ref, q),
-        (kc_ref, kb.at[pl.ds(0, POOL)]), (vc_ref, vb.at[pl.ds(0, POOL)]),
-        (li_ref, li), (gain_ref, gain),
-        (wg_ref, wgu.at[pl.ds(0, width)]), (wu_ref, wgu.at[pl.ds(width, width)]), (wd_ref, wd),
-    )
-    loads = [pltpu.make_async_copy(src, dst, lsem.at[i]) for i, (src, dst) in enumerate(moves)]
-    for load in loads[:10]:
-        load.start()
+    pool, pairs = pl.ds(0, POOL), [pl.ds(2 * HD * p, 2 * HD) for p in range(2)]
+    moves = {
+        "k0": (kc_ref.at[:, pairs[0]], kb.at[pool, pairs[0]]),
+        "q": (q_ref, q),
+        "pt": (pt_in, pt),
+        "cl": (cl_in, cl),
+        "nk": (nk_ref, nk),
+        "v0": (vc_ref.at[:, pairs[0]], vb.at[pool, pairs[0]]),
+        "nv": (nv_ref, nv),
+        "li": (li_ref, li),
+        "gain": (gain_ref, gain),
+        "k1": (kc_ref.at[:, pairs[1]], kb.at[pool, pairs[1]]),
+        "v1": (vc_ref.at[:, pairs[1]], vb.at[pool, pairs[1]]),
+        "bs": (bs_in, bs),
+        "wg": (wg_ref, wgu.at[pl.ds(0, width)]),
+        "wu": (wu_ref, wgu.at[pl.ds(width, width)]),
+        "wd": (wd_ref, wd),
+    }
+    loads = {
+        name: pltpu.make_async_copy(src, dst, lsem.at[i])
+        for i, (name, (src, dst)) in enumerate(moves.items())
+    }
+    for name in list(moves)[:12]:
+        loads[name].start()
+
+    def lanes(j):
+        return pl.ds(j * W, W)
+
+    def sent_lanes(j):
+        return pl.ds(j * W, W + SCALE if j == NJ - 1 else W)
+
+    def ag(src, dst, j, dev):
+        return remote(
+            gath.at[0, src, :, sent_lanes(j)], gath.at[0, dst, :, sent_lanes(j)],
+            ag_send.at[0], ag_recv.at[dst, j], dev,
+        )
+
+    groups = ((0, 1), (1, 4), (5, 4), (9, 4), (13, 3))
+
+    def ag_sib(group, j):
+        part = pl.ds(*groups[group])
+        return remote(
+            gath.at[0, part, :, sent_lanes(j)], gath.at[1, part, :, sent_lanes(j)],
+            as_send.at[0], as_recv.at[group, j], sib,
+        )
+
+    def goes(m, j, sign):
+        return m < 8 or (j < NJ // 2) == (sign > 0)
+
+    def spread(m, j):
+        for n in children(m):
+            for sign, devices in ((1, right), (-1, left)):
+                if goes(n, j, sign):
+                    ag(slot_of(-sign * m), slot_of(-sign * n), j, devices[n - m]).start()
+
+    def arrive(m, j):
+        for sign in (1, -1):
+            if goes(m, j, sign):
+                ag(0, slot_of(-sign * m), j, right[1]).wait_recv()
 
     def stacked(ref, width):
         for s in range(4):
             rows[2 * s : 2 * s + 2, :width] = ref[s].astype(jnp.float32)
         return rows[:, :width]
 
-    for load in loads[:3]:
-        load.wait()
+    loads["pt"].wait()
+    loads["cl"].wait()
     col1 = lax.broadcasted_iota(jnp.int32, (1, KEYS), 1)
     page = lax.shift_right_logical(col1, 5)
     off = jnp.bitwise_and(col1, 31)
@@ -107,19 +157,18 @@
     )
     bias = jnp.where(fresh, 0.0, bias)
 
-    for load in loads[3:5]:
-        load.wait()
+    loads["q"].wait()
+    qf = stacked(q, D)
+    loads["nk"].wait()
+    loads["nv"].wait()
     zeros8 = jnp.zeros((8, KVH * HD), jnp.float32)
     kb[pl.ds(POOL, 16)] = jnp.concatenate([stacked(nk, KVH * HD), zeros8], 0).astype(jnp.bfloat16)
     vb[pl.ds(POOL, 16)] = jnp.concatenate([stacked(nv, KVH * HD), zeros8], 0).astype(jnp.bfloat16)
     kb[pl.ds(POOL + 16, 112)] = jnp.zeros((112, KVH * HD), jnp.bfloat16)
     vb[pl.ds(POOL + 16, 112)] = jnp.zeros((112, KVH * HD), jnp.bfloat16)
-    loads[5].wait()
-    qf = stacked(q, D)
     scale = 1.0 / jnp.sqrt(jnp.float32(HD))
-    loads[6].wait()
-    heads = []
     blank = jnp.zeros((64, HD), jnp.float32)
+    squares = jnp.zeros((8, 1), jnp.float32)
     for pair in range(KVH // 2):
         both = [
             jnp.concatenate(
@@ -131,6 +180,7 @@
             [jnp.concatenate([both[0], blank], 1), jnp.concatenate([blank, both[1]], 1)], 0
         ).astype(jnp.bfloat16)
         place = slice(2 * pair * HD, 2 * (pair + 1) * HD)
+        loads[("k0", "k1")[pair]].wait()
         scores = lax.dot_general(
             both, kb[:, place], (((1,), (1,)), ((), ())), preferred_element_type=jnp.float32
         )
@@ -138,67 +188,44 @@
         highest = jnp.max(scores, axis=-1, keepdims=True)
         expo = jnp.exp(scores - highest)
         total = jnp.sum(expo, axis=-1, keepdims=True)
-        if pair == 0:
-            loads[7].wait()
-            for load in loads[10:]:
-                load.start()
+        loads[("v0", "v1")[pair]].wait()
         mixed = jnp.dot(
             expo.astype(jnp.bfloat16), vb[:, place], preferred_element_type=jnp.float32
         ) / total
-        for i in range(2):
-            heads += [
-                mixed[64 * i + 8 * g : 64 * i + 8 * g + 8, i * HD : (i + 1) * HD] for g in range(8)
-            ]
-    attention = jnp.concatenate(heads, 1).astype(jnp.bfloat16).astype(jnp.float32)
-    loads[8].wait()
-    residual = stacked(li, D) + attention
-    res[...] = residual
-    inverse = lax.rsqrt(jnp.mean(residual * residual, axis=-1, keepdims=True) + eps)
-    loads[9].wait()
-    normed = residual * inverse * gain[...]
-    live = jnp.bitwise_and(lax.broadcasted_iota(jnp.int32, (8, D), 0), 1) < bs[0]
-    normed = jnp.where(live, normed, 0.0)
-    for c in range(NC):
-        both = [normed[:, (2 * c + fold) * CW : (2 * c + fold + 1) * CW] for fold in range(2)]
-        gath[0, 0, :, c * CW : (c + 1) * CW] = jnp.concatenate(both, 0).astype(jnp.bfloat16)
-    pl.semaphore_wait(barrier, len(partners))
-
-    def lanes(j):
-        return pl.ds(j * W, W)
-
-    def ag(src, dst, j, dev):
-        return remote(
-            gath.at[0, src, :, lanes(j)], gath.at[0, dst, :, lanes(j)],
-            ag_send.at[0], ag_recv.at[dst, j], dev,
-        )
-
-    groups = ((0, 1), (1, 4), (5, 4), (9, 4), (13, 3))
-
-    def ag_sib(group, j):
-        part = pl.ds(*groups[group])
-        return remote(
-            gath.at[0, part, :, lanes(j)], gath.at[1, part, :, lanes(j)],
-            as_send.at[0], as_recv.at[group, j], sib,
-        )
-
-    def goes(m, j, sign):
-        return m < 8 or (j < NJ // 2) == (sign > 0)
-
-    def spread(m, j):
-        for n in children(m):
-            for sign, devices in ((1, right), (-1, left)):
-                if goes(n, j, sign):
-                    ag(slot_of(-sign * m), slot_of(-sign * n), j, devices[n - m]).start()
-
-    def arrive(m, j):
-        for sign in (1, -1):
-            if goes(m, j, sign):
-                ag(0, slot_of(-sign * m), j, right[1]).wait_recv()
-
-    for j in range(NJ):
-        spread(0, j)
-    for j in range(NJ):
-        ag_sib(0, j).start()
+        attention = jnp.concatenate(
+            [
+                mixed[64 * i + 8 * g : 64 * i + 8 * g + 8, i * HD : (i + 1) * HD]
+                for i in range(2)
+                for g in range(8)
+            ],
+            1,
+        ).astype(jnp.bfloat16).astype(jnp.float32)
+        if pair == 0:
+            loads["li"].wait()
+            inputs = stacked(li, D)
+            loads["gain"].wait()
+        mine = slice(pair * D // 2, (pair + 1) * D // 2)
+        residual = inputs[:, mine] + attention
+        res[:, mine] = residual
+        squares += jnp.sum(residual * residual, axis=-1, keepdims=True)
+        row = residual * gain[:, mine]
+        for c in range(NC // NJ):
+            both = [row[:, (2 * c + fold) * CW : (2 * c + fold + 1) * CW] for fold in range(2)]
+            start = pair * W + c * CW
+            gath[0, 0, :, start : start + CW] = jnp.concatenate(both, 0).astype(jnp.bfloat16)
+        if pair == 0:
+            pl.semaphore_wait(barrier, len(partners))
+        else:
+            loads["bs"].wait()
+            row_scale = jnp.broadcast_to(lax.rsqrt(squares / D + eps), (8, SCALE))
+            live = jnp.bitwise_and(lax.broadcasted_iota(jnp.int32, (8, SCALE), 0), 1) < bs[0]
+            row_scale = jnp.where(live, row_scale, 0.0)
+            high = row_scale.astype(jnp.bfloat16).astype(jnp.float32)
+            gath[0, 0, :, 2 * W :] = jnp.concatenate([high, row_scale - high], 0).astype(jnp.bfloat16)
+        spread(0, pair)
+        ag_sib(0, pair).start()
+    for name in ("wg", "wu", "wd"):
+        loads[name].start()
 
     def piece(c):
         return pl.ds(c * CW, CW)
@@ -227,8 +254,11 @@
             acc[half] += term
 
     def activate(half):
-        gate = acc[half, :width]
-        value = gate / (1.0 + jnp.exp(-gate)) * acc[half, width:]
+        parts = gath[:, pl.ds(half * 8, 8), :, pl.ds(2 * W, SCALE)].astype(jnp.float32)
+        parts = parts.reshape(16, 2, 8, SCALE)
+        row_scale = (parts[:, 0] + parts[:, 1]).reshape(128, SCALE).T[:1]
+        gate = acc[half, :width] * row_scale
+        value = gate / (1.0 + jnp.exp(-gate)) * (acc[half, width:] * row_scale)
         hid[half] = value.T.astype(jnp.bfloat16)
 
     def sib_sum(half, c):
@@ -294,12 +324,12 @@
 
     for group in range(3):
         gathered(group)
-    loads[10].wait()
-    loads[11].wait()
+    loads["wg"].wait()
+    loads["wu"].wait()
     for j in range(NJ):
         gate_up(0, j)
     activate(0)
-    loads[12].wait()
+    loads["wd"].wait()
     down(0)
 
     for j in range(NJ):
@@ -384,7 +414,7 @@
             pltpu.VMEM((width, D), bf16),
             pltpu.VMEM((8, D), f32),
             pltpu.VMEM((8, D), f32),
-            pltpu.VMEM((2, 16, 16, HALF), bf16),
+            pltpu.VMEM((2, 16, 16, HALF + SCALE), bf16),
             pltpu.VMEM((2, 2 * width, 128), f32),
             pltpu.VMEM((2, 128, width), bf16),
             pltpu.VMEM((16, 16, HALF), f32),
@@ -394,7 +424,7 @@
             pltpu.VMEM((8, 16, HALF), bf16),
             pltpu.VMEM((8, 16, HALF), bf16),
             pltpu.VMEM((8, 16, HALF), bf16),
-            dma((13,)),
+            dma((15,)),
             dma((1,)),
             dma((16, NJ)),
             dma((1,)),

time: 60.6 us -> 60.2 us (level)
  no operation moved by 1% of the time
where the time goes in v3:
time: 60.2 us; the launch traced here: 60 us
  Pallas kernels  58.6 us (97%)
  local copies, waits for them, and re-layouts  0.69 us (1%)
  between operations  0.66 us (1%)
    pallas_call x1, Pallas kernels, local(): pl.pallas_call(kernel, out_shape=pltpu.VMEM((8, D), bf16), in_specs=[hbm]...  58.6 us

profile of v3, /device:TPU:24, one launch (start us, length us, event | category | flops | bytes accessed | tf_op | source)
XLA Modules:
  0.0 60.0 jit_solution(11658170397831560006)
XLA Ops:
  0.7 58.6 %shard_map.127 = bf16[8,4096]{1,0:T(8,128)(2,1)S(1)} custom-call(s32[1]{0:T(128)S(6)} %copy.14.bs_in, s32[2]{0:T(128)} %cl_in.1, s32[2,16]{1,0:T(2,128)} %pt_in.1, bf16[4,2,4096]{2,1,0:T(2,128)(2,1)} %li_ref.1, bf16[4,2,4096]{2,1,0:T(2,128)(2,1)} %q_ref.1, bf16[4,2,512]{2,1,0:T(2,128)(2,1)} %nk_ref.1, bf16[4,2,512]{2,1,0:T(2,128)(2,1)} %nv_ref.1, ...), custom_call_target="tpu_custom_call" | custom-call | tf_op jit(solution)/shard_map/pallas_call | solution.py:397
  59.3 0.7 %reshape.15 = bf16[4,2,4096]{2,1,0:T(2,128)(2,1)} reshape(bf16[8,4096]{1,0:T(8,128)(2,1)S(1)} %shard_map.127) | data formatting | bytes 131072 | tf_op jit(solution)/shard_map/reshape | solution.py:457

commit v4 on v3

--- a/solution.py
+++ b/solution.py
@@ -15,7 +15,7 @@
 SCALE = 128
 NC = 4
 CW = HALF // NC
-CHIPS = 16
+REPS = 16
 POOL = 1024
 KEYS = POOL + 128
 
@@ -28,7 +28,7 @@
 
 masked = -1e30
 eps = 1e-05
-MESH = pl.DeviceIdType.MESH
+LOGICAL = pl.DeviceIdType.LOGICAL
 
 
 def slot_of(offset):
@@ -46,23 +46,26 @@
     lsem, ag_send, ag_recv, as_send, as_recv,
     ps_send, ps_recv, ms_send, ms_recv, ss_send, ss_recv,
 ):
-    me = lax.axis_index("dp")
-    core = lax.rem(me, 2)
+    me, rep = lax.axis_index("dp"), lax.axis_index("rep")
+
+    def place(dp):
+        return dp * REPS + rep
+
     steps = sorted({n - m for n, m in PARENT.items()})
-    right = {step: lax.rem(me + 2 * step, 32) for step in steps}
-    left = {step: lax.rem(me + 32 - 2 * step, 32) for step in steps}
-    sib = me + 1 - 2 * core
+    right = {step: place(lax.rem(me + 2 * step, 32)) for step in steps}
+    left = {step: place(lax.rem(me + 32 - 2 * step, 32)) for step in steps}
+    sib = place(me + 1 - 2 * lax.rem(me, 2))
 
     def remote(src, dst, send, recv, dev):
         return pltpu.make_async_remote_copy(
             src_ref=src, dst_ref=dst, send_sem=send, recv_sem=recv,
-            device_id={"dp": dev}, device_id_type=MESH,
+            device_id=dev, device_id_type=LOGICAL,
         )
 
     barrier = pltpu.get_barrier_semaphore()
     partners = [*left.values(), *right.values(), sib]
     for dev in partners:
-        pl.semaphore_signal(barrier, inc=1, device_id={"dp": dev}, device_id_type=MESH)
+        pl.semaphore_signal(barrier, inc=1, device_id=dev, device_id_type=LOGICAL)
 
     width = wd.shape[0]
     pool, pairs = pl.ds(0, POOL), [pl.ds(2 * HD * p, 2 * HD) for p in range(2)]
@@ -87,8 +90,8 @@
         name: pltpu.make_async_copy(src, dst, lsem.at[i])
         for i, (name, (src, dst)) in enumerate(moves.items())
     }
-    for name in list(moves)[:12]:
-        loads[name].start()
+    for load in loads.values():
+        load.start()
 
     def lanes(j):
         return pl.ds(j * W, W)
@@ -179,10 +182,10 @@
         both = jnp.concatenate(
             [jnp.concatenate([both[0], blank], 1), jnp.concatenate([blank, both[1]], 1)], 0
         ).astype(jnp.bfloat16)
-        place = slice(2 * pair * HD, 2 * (pair + 1) * HD)
+        these = slice(2 * pair * HD, 2 * (pair + 1) * HD)
         loads[("k0", "k1")[pair]].wait()
         scores = lax.dot_general(
-            both, kb[:, place], (((1,), (1,)), ((), ())), preferred_element_type=jnp.float32
+            both, kb[:, these], (((1,), (1,)), ((), ())), preferred_element_type=jnp.float32
         )
         scores = (scores.reshape(16, 8, KEYS) * scale + bias[None]).reshape(128, KEYS)
         highest = jnp.max(scores, axis=-1, keepdims=True)
@@ -190,7 +193,7 @@
         total = jnp.sum(expo, axis=-1, keepdims=True)
         loads[("v0", "v1")[pair]].wait()
         mixed = jnp.dot(
-            expo.astype(jnp.bfloat16), vb[:, place], preferred_element_type=jnp.float32
+            expo.astype(jnp.bfloat16), vb[:, these], preferred_element_type=jnp.float32
         ) / total
         attention = jnp.concatenate(
             [
@@ -224,9 +227,6 @@
             gath[0, 0, :, 2 * W :] = jnp.concatenate([high, row_scale - high], 0).astype(jnp.bfloat16)
         spread(0, pair)
         ag_sib(0, pair).start()
-    for name in ("wg", "wu", "wd"):
-        loads[name].start()
-
     def piece(c):
         return pl.ds(c * CW, CW)
 

time: 60.2 us -> 60.2 us (level)
  no operation moved by 1% of the time
where the time goes in v4:
time: 60.2 us; the launch traced here: 59.4 us
  Pallas kernels  58 us (96%)
  local copies, waits for them, and re-layouts  0.69 us (1%)
  between operations  0.66 us (1%)
    pallas_call x1, Pallas kernels, local(): pl.pallas_call(kernel, out_shape=pltpu.VMEM((8, D), bf16), in_specs=[hbm]...  58 us

profile of v4, /device:TPU:24, one launch (start us, length us, event | category | flops | bytes accessed | tf_op | source)
XLA Modules:
  0.0 59.4 jit_solution(12366056527100951744)
XLA Ops:
  0.7 58.0 %shard_map.127 = bf16[8,4096]{1,0:T(8,128)(2,1)S(1)} custom-call(s32[1]{0:T(128)S(6)} %copy.14.bs_in, s32[2]{0:T(128)} %cl_in.1, s32[2,16]{1,0:T(2,128)} %pt_in.1, bf16[4,2,4096]{2,1,0:T(2,128)(2,1)} %li_ref.1, bf16[4,2,4096]{2,1,0:T(2,128)(2,1)} %q_ref.1, bf16[4,2,512]{2,1,0:T(2,128)(2,1)} %nk_ref.1, bf16[4,2,512]{2,1,0:T(2,128)(2,1)} %nv_ref.1, ...), custom_call_target="tpu_custom_call" | custom-call | tf_op jit(solution)/shard_map/pallas_call | solution.py:397
  58.7 0.7 %reshape.15 = bf16[4,2,4096]{2,1,0:T(2,128)(2,1)} reshape(bf16[8,4096]{1,0:T(8,128)(2,1)S(1)} %shard_map.127) | data formatting | bytes 131072 | tf_op jit(solution)/shard_map/reshape | solution.py:457

commit v5 on v4

--- a/solution.py
+++ b/solution.py
@@ -41,10 +41,9 @@
     bs_in, cl_in, pt_in, li_ref, q_ref, nk_ref, nv_ref, gain_ref,
     kc_ref, vc_ref, wg_ref, wu_ref, wd_ref,
     out_ref,
-    bs, cl, pt, li, q, nk, nv, gain, kb, vb, wgu, wd, rows, res, gath, acc, hid, own, sibs, sibr,
+    bs, cl, pt, li, q, nk, nv, gain, kb, vb, wgu, wd, rows, res, gath, acc, hid, own,
     sp, sm, rp, rm,
-    lsem, ag_send, ag_recv, as_send, as_recv,
-    ps_send, ps_recv, ms_send, ms_recv, ss_send, ss_recv,
+    lsem, w_send, w_recv, ag_send, ag_recv, ps_send, ps_recv, ms_send, ms_recv,
 ):
     me, rep = lax.axis_index("dp"), lax.axis_index("rep")
 
@@ -67,7 +66,7 @@
     for dev in partners:
         pl.semaphore_signal(barrier, inc=1, device_id=dev, device_id_type=LOGICAL)
 
-    width = wd.shape[0]
+    width = wd.shape[0] // 2
     pool, pairs = pl.ds(0, POOL), [pl.ds(2 * HD * p, 2 * HD) for p in range(2)]
     moves = {
         "k0": (kc_ref.at[:, pairs[0]], kb.at[pool, pairs[0]]),
@@ -84,7 +83,7 @@
         "bs": (bs_in, bs),
         "wg": (wg_ref, wgu.at[pl.ds(0, width)]),
         "wu": (wu_ref, wgu.at[pl.ds(width, width)]),
-        "wd": (wd_ref, wd),
+        "wd": (wd_ref, wd.at[pl.ds(0, width)]),
     }
     loads = {
         name: pltpu.make_async_copy(src, dst, lsem.at[i])
@@ -93,6 +92,20 @@
     for load in loads.values():
         load.start()
 
+    pl.semaphore_wait(barrier, len(partners))
+    pushes = []
+    for part in range(2):
+        columns = pl.ds(part * D // 2, D // 2)
+        for k, (src, full) in enumerate(((wg_ref, wgu), (wu_ref, wgu), (wd_ref, wd))):
+            dst = full.at[pl.ds((2 + k) * width if k < 2 else width, width), columns]
+            pushes.append((src.at[:, columns], dst))
+    order = (0, 1, 3, 4, 2, 5)
+    pushes = [
+        remote(*pushes[k], w_send.at[i], w_recv.at[i], sib) for i, k in enumerate(order)
+    ]
+    for push in pushes:
+        push.start()
+
     def lanes(j):
         return pl.ds(j * W, W)
 
@@ -101,17 +114,8 @@
 
     def ag(src, dst, j, dev):
         return remote(
-            gath.at[0, src, :, sent_lanes(j)], gath.at[0, dst, :, sent_lanes(j)],
+            gath.at[src, :, sent_lanes(j)], gath.at[dst, :, sent_lanes(j)],
             ag_send.at[0], ag_recv.at[dst, j], dev,
-        )
-
-    groups = ((0, 1), (1, 4), (5, 4), (9, 4), (13, 3))
-
-    def ag_sib(group, j):
-        part = pl.ds(*groups[group])
-        return remote(
-            gath.at[0, part, :, sent_lanes(j)], gath.at[1, part, :, sent_lanes(j)],
-            as_send.at[0], as_recv.at[group, j], sib,
         )
 
     def goes(m, j, sign):
@@ -215,27 +219,23 @@
         for c in range(NC // NJ):
             both = [row[:, (2 * c + fold) * CW : (2 * c + fold + 1) * CW] for fold in range(2)]
             start = pair * W + c * CW
-            gath[0, 0, :, start : start + CW] = jnp.concatenate(both, 0).astype(jnp.bfloat16)
-        if pair == 0:
-            pl.semaphore_wait(barrier, len(partners))
-        else:
+            gath[0, :, start : start + CW] = jnp.concatenate(both, 0).astype(jnp.bfloat16)
+        if pair == 1:
             loads["bs"].wait()
             row_scale = jnp.broadcast_to(lax.rsqrt(squares / D + eps), (8, SCALE))
             live = jnp.bitwise_and(lax.broadcasted_iota(jnp.int32, (8, SCALE), 0), 1) < bs[0]
             row_scale = jnp.where(live, row_scale, 0.0)
             high = row_scale.astype(jnp.bfloat16).astype(jnp.float32)
-            gath[0, 0, :, 2 * W :] = jnp.concatenate([high, row_scale - high], 0).astype(jnp.bfloat16)
+            gath[0, :, 2 * W :] = jnp.concatenate([high, row_scale - high], 0).astype(jnp.bfloat16)
         spread(0, pair)
-        ag_sib(0, pair).start()
     def piece(c):
         return pl.ds(c * CW, CW)
 
     def features(c):
         return pl.ds(c * 2 * CW, 2 * CW)
 
-    def gate_up(half, j):
-        block = gath[:, pl.ds(half * 8, 8), :, lanes(j)].astype(jnp.float32)
-        block = block.reshape(16, 2, 8, W)
+    def gate_up(j):
+        block = gath[:, :, lanes(j)].astype(jnp.float32).reshape(16, 2, 8, W)
         block = jnp.concatenate(
             [
                 block[:, fold, :, c * CW : (c + 1) * CW].reshape(128, CW)
@@ -249,39 +249,29 @@
             (((1,), (1,)), ((), ())), preferred_element_type=jnp.float32,
         )
         if j == 0:
-            acc[half] = term
+            acc[...] = term
         else:
-            acc[half] += term
-
-    def activate(half):
-        parts = gath[:, pl.ds(half * 8, 8), :, pl.ds(2 * W, SCALE)].astype(jnp.float32)
-        parts = parts.reshape(16, 2, 8, SCALE)
+            acc[...] += term
+
+    def activate():
+        parts = gath[:, :, pl.ds(2 * W, SCALE)].astype(jnp.float32).reshape(16, 2, 8, SCALE)
         row_scale = (parts[:, 0] + parts[:, 1]).reshape(128, SCALE).T[:1]
-        gate = acc[half, :width] * row_scale
-        value = gate / (1.0 + jnp.exp(-gate)) * (acc[half, width:] * row_scale)
-        hid[half] = value.T.astype(jnp.bfloat16)
-
-    def sib_sum(half, c):
-        slots = pl.ds(half * 8, 8)
-        return remote(
-            sibs.at[slots, :, piece(c)], sibr.at[slots, :, piece(c)],
-            ss_send.at[0], ss_recv.at[half, c], sib,
-        )
-
-    def down(half):
-        def step(c, carry):
-            term = jnp.dot(hid[half], wd[:, features(c)], preferred_element_type=jnp.float32)
-            both = [
-                term[:, fold * CW : (fold + 1) * CW].reshape(2, 8, 1, 8, CW) for fold in range(2)
-            ]
-            both = jnp.concatenate(both, 2).reshape(2, 8, 16, CW)
-            slots = pl.ds(half * 8, 8)
-            sibs[slots, :, piece(c)] = both[1].astype(jnp.bfloat16)
-            sib_sum(half, c).start()
-            own[slots, :, piece(c)] = both[0]
-            return carry
-
-        lax.fori_loop(0, NC, step, 0)
+        for core in range(2):
+            gate = acc[2 * core * width : (2 * core + 1) * width] * row_scale
+            upward = acc[(2 * core + 1) * width : (2 * core + 2) * width] * row_scale
+            value = gate / (1.0 + jnp.exp(-gate)) * upward
+            hid[core] = value.T.astype(jnp.bfloat16)
+
+    def down(c):
+        term = sum(
+            jnp.dot(
+                hid[core], wd[pl.ds(core * width, width), features(c)],
+                preferred_element_type=jnp.float32,
+            )
+            for core in range(2)
+        )
+        both = [term[:, fold * CW : (fold + 1) * CW].reshape(16, 1, 8, CW) for fold in range(2)]
+        own[:, :, piece(c)] = jnp.concatenate(both, 1).reshape(16, 16, CW)
 
     def plus(m, j):
         return remote(
@@ -302,7 +292,7 @@
             if not goes(m, j, sign):
                 continue
             slot = slot_of(sign * m)
-            value = own[slot, :, lanes(j)] + sibr[slot, :, lanes(j)].astype(jnp.float32)
+            value = own[slot, :, lanes(j)]
             for source in children(m):
                 if goes(source, j, sign):
                     copy(source, j).wait_recv()
@@ -310,51 +300,27 @@
             leaving[m - 1, :, lanes(j)] = value.astype(jnp.bfloat16)
             copy(m, j).start()
 
-    def gathered(group):
+    for m in (2, 1, 4, 3, 6, 5):
         for j in range(NJ):
-            ag_sib(group, j).wait_recv()
-
-    for stage in range(1, 4):
-        for j in range(NJ):
-            arrive(2 * stage, j)
-            spread(2 * stage, j)
-        for j in range(NJ):
-            arrive(2 * stage - 1, j)
-            ag_sib(stage, j).start()
-
-    for group in range(3):
-        gathered(group)
-    loads["wg"].wait()
-    loads["wu"].wait()
-    for j in range(NJ):
-        gate_up(0, j)
-    activate(0)
-    loads["wd"].wait()
-    down(0)
-
+            arrive(m, j)
+            spread(m, j)
+    for name in ("wg", "wu"):
+        loads[name].wait()
     for j in range(NJ):
         arrive(7, j)
         arrive(8, j)
-        ag_sib(4, j).start()
-    for c in range(NC):
-        sib_sum(0, c).wait_recv()
+        for push in pushes[2 * j : 2 * j + 2]:
+            push.wait_recv()
+        gate_up(j)
+    activate()
+    loads["wd"].wait()
     for j in range(NJ):
-        pass_on(3, j)
-
-    for j in range(NJ):
-        for group in (3, 4):
-            ag_sib(group, j).wait_recv()
-        gate_up(1, j)
-    activate(1)
-    down(1)
-    for j in range(NJ):
-        pass_on(1, j)
-    for j in range(NJ):
+        pushes[4 + j].wait_recv()
         for c in range(j * NC // NJ, (j + 1) * NC // NJ):
-            sib_sum(1, c).wait_recv()
+            down(c)
         for m in (8, 7):
             pass_on(m, j)
-    for m in (5, 6, 4, 2):
+    for m in (5, 6, 3, 4, 1, 2):
         for j in range(NJ):
             pass_on(m, j)
 
@@ -364,7 +330,7 @@
             plus(m, j).wait_recv()
             minus(m, j).wait_recv()
         for c in range(j * NC // NJ, (j + 1) * NC // NJ):
-            value = own[0, :, piece(c)] + sibr[0, :, piece(c)].astype(jnp.float32)
+            value = own[0, :, piece(c)]
             for m in children(0):
                 for arrived in (rp, rm):
                     value = value + arrived[m - 1, :, piece(c)].astype(jnp.float32)
@@ -376,9 +342,9 @@
     def sent(part, sem):
         remote(part, part, sem, sem, sib).wait_send()
 
-    sent(gath.at[0, pl.ds(1, 15)], ag_send.at[0])
-    sent(gath.at[0], as_send.at[0])
-    sent(sibs, ss_send.at[0])
+    for push in pushes:
+        push.wait_send()
+    sent(gath.at[pl.ds(1, 15)], ag_send.at[0])
     sent(sp.at[7, :, pl.ds(0, HALF // 2)], ps_send.at[1])
     sent(sm.at[7, :, pl.ds(0, HALF // 2)], ms_send.at[1])
     sent(sp.at[pl.ds(0, 7)], ps_send.at[0])
@@ -410,31 +376,27 @@
             pltpu.VMEM((1, D), f32),
             pltpu.VMEM((KEYS, KVH * HD), bf16),
             pltpu.VMEM((KEYS, KVH * HD), bf16),
+            pltpu.VMEM((4 * width, D), bf16),
             pltpu.VMEM((2 * width, D), bf16),
-            pltpu.VMEM((width, D), bf16),
             pltpu.VMEM((8, D), f32),
             pltpu.VMEM((8, D), f32),
-            pltpu.VMEM((2, 16, 16, HALF + SCALE), bf16),
-            pltpu.VMEM((2, 2 * width, 128), f32),
+            pltpu.VMEM((16, 16, HALF + SCALE), bf16),
+            pltpu.VMEM((4 * width, 128), f32),
             pltpu.VMEM((2, 128, width), bf16),
             pltpu.VMEM((16, 16, HALF), f32),
-            pltpu.VMEM((16, 16, HALF), bf16),
-            pltpu.VMEM((16, 16, HALF), bf16),
             pltpu.VMEM((8, 16, HALF), bf16),
             pltpu.VMEM((8, 16, HALF), bf16),
             pltpu.VMEM((8, 16, HALF), bf16),
             pltpu.VMEM((8, 16, HALF), bf16),
             dma((15,)),
+            dma((6,)),
+            dma((6,)),
             dma((1,)),
             dma((16, NJ)),
-            dma((1,)),
-            dma((5, NJ)),
             dma((2,)),
             dma((8, NJ)),
             dma((2,)),
             dma((8, NJ)),
-            dma((1,)),
-            dma((2, NC)),
         ],
         compiler_params=pltpu.CompilerParams(
             collective_id=0, has_side_effects=True, vmem_limit_bytes=56 * 1024 * 1024

time: 60.2 us -> 60.4 us (level); the launches traced: 59.4 us -> 60.2 us
  Pallas kernels: 58 us -> 58.9 us
    pallas_call x1, Pallas kernels: 58 us -> 58.9 us  [local(): pl.pallas_call(kernel, out_shape=pltpu.VMEM((8, D), bf16), in_specs=[hbm]...]
where the time goes in v5:
time: 60.4 us; the launch traced here: 60.2 us
  Pallas kernels  58.9 us (98%)
  local copies, waits for them, and re-layouts  0.69 us (1%)
  between operations  0.66 us (1%)
    pallas_call x1, Pallas kernels, local(): pl.pallas_call(kernel, out_shape=pltpu.VMEM((8, D), bf16), in_specs=[hbm]...  58.9 us

profile of v5, /device:TPU:24, one launch (start us, length us, event | category | flops | bytes accessed | tf_op | source)
XLA Modules:
  0.0 60.2 jit_solution(5541767164775076185)
XLA Ops:
  0.7 58.9 %shard_map.127 = bf16[8,4096]{1,0:T(8,128)(2,1)S(1)} custom-call(s32[1]{0:T(128)S(6)} %copy.14.bs_in, s32[2]{0:T(128)} %cl_in.1, s32[2,16]{1,0:T(2,128)} %pt_in.1, bf16[4,2,4096]{2,1,0:T(2,128)(2,1)} %li_ref.1, bf16[4,2,4096]{2,1,0:T(2,128)(2,1)} %q_ref.1, bf16[4,2,512]{2,1,0:T(2,128)(2,1)} %nk_ref.1, bf16[4,2,512]{2,1,0:T(2,128)(2,1)} %nv_ref.1, ...), custom_call_target="tpu_custom_call" | custom-call | tf_op jit(solution)/shard_map/pallas_call | solution.py:363
  59.5 0.7 %reshape.15 = bf16[4,2,4096]{2,1,0:T(2,128)(2,1)} reshape(bf16[8,4096]{1,0:T(8,128)(2,1)S(1)} %shard_map.127) | data formatting | bytes 131072 | tf_op jit(solution)/shard_map/reshape | solution.py:419

commit v6 on v5

--- a/solution.py
+++ b/solution.py
@@ -10,7 +10,7 @@
 KVH = 4
 HD = 128
 HALF = D // 2
-NJ = 2
+NJ = 4
 W = HALF // NJ
 SCALE = 128
 NC = 4
@@ -117,6 +117,9 @@
             gath.at[src, :, sent_lanes(j)], gath.at[dst, :, sent_lanes(j)],
             ag_send.at[0], ag_recv.at[dst, j], dev,
         )
+
+    def chunks(h):
+        return range(h * NJ // 2, (h + 1) * NJ // 2)
 
     def goes(m, j, sign):
         return m < 8 or (j < NJ // 2) == (sign > 0)
@@ -216,9 +219,9 @@
         res[:, mine] = residual
         squares += jnp.sum(residual * residual, axis=-1, keepdims=True)
         row = residual * gain[:, mine]
-        for c in range(NC // NJ):
+        for c in range(NC // 2):
             both = [row[:, (2 * c + fold) * CW : (2 * c + fold + 1) * CW] for fold in range(2)]
-            start = pair * W + c * CW
+            start = pair * HALF // 2 + c * CW
             gath[0, :, start : start + CW] = jnp.concatenate(both, 0).astype(jnp.bfloat16)
         if pair == 1:
             loads["bs"].wait()
@@ -226,35 +229,37 @@
             live = jnp.bitwise_and(lax.broadcasted_iota(jnp.int32, (8, SCALE), 0), 1) < bs[0]
             row_scale = jnp.where(live, row_scale, 0.0)
             high = row_scale.astype(jnp.bfloat16).astype(jnp.float32)
-            gath[0, :, 2 * W :] = jnp.concatenate([high, row_scale - high], 0).astype(jnp.bfloat16)
-        spread(0, pair)
+            gath[0, :, HALF:] = jnp.concatenate([high, row_scale - high], 0).astype(jnp.bfloat16)
+        for j in chunks(pair):
+            spread(0, j)
     def piece(c):
         return pl.ds(c * CW, CW)
 
     def features(c):
         return pl.ds(c * 2 * CW, 2 * CW)
 
-    def gate_up(j):
-        block = gath[:, :, lanes(j)].astype(jnp.float32).reshape(16, 2, 8, W)
+    def gate_up(h):
+        block = gath[:, :, pl.ds(h * HALF // 2, HALF // 2)].astype(jnp.float32)
+        block = block.reshape(16, 2, 8, HALF // 2)
         block = jnp.concatenate(
             [
                 block[:, fold, :, c * CW : (c + 1) * CW].reshape(128, CW)
-                for c in range(NC // NJ)
+                for c in range(NC // 2)
                 for fold in range(2)
             ],
             1,
         )
         term = lax.dot_general(
-            wgu[:, pl.ds(j * 2 * W, 2 * W)], block.astype(jnp.bfloat16),
+            wgu[:, pl.ds(h * D // 2, D // 2)], block.astype(jnp.bfloat16),
             (((1,), (1,)), ((), ())), preferred_element_type=jnp.float32,
         )
-        if j == 0:
+        if h == 0:
             acc[...] = term
         else:
             acc[...] += term
 
     def activate():
-        parts = gath[:, :, pl.ds(2 * W, SCALE)].astype(jnp.float32).reshape(16, 2, 8, SCALE)
+        parts = gath[:, :, pl.ds(HALF, SCALE)].astype(jnp.float32).reshape(16, 2, 8, SCALE)
         row_scale = (parts[:, 0] + parts[:, 1]).reshape(128, SCALE).T[:1]
         for core in range(2):
             gate = acc[2 * core * width : (2 * core + 1) * width] * row_scale
@@ -306,20 +311,22 @@
             spread(m, j)
     for name in ("wg", "wu"):
         loads[name].wait()
-    for j in range(NJ):
-        arrive(7, j)
-        arrive(8, j)
-        for push in pushes[2 * j : 2 * j + 2]:
+    for h in range(2):
+        for j in chunks(h):
+            arrive(7, j)
+            arrive(8, j)
+        for push in pushes[2 * h : 2 * h + 2]:
             push.wait_recv()
-        gate_up(j)
+        gate_up(h)
     activate()
     loads["wd"].wait()
-    for j in range(NJ):
-        pushes[4 + j].wait_recv()
-        for c in range(j * NC // NJ, (j + 1) * NC // NJ):
-            down(c)
-        for m in (8, 7):
-            pass_on(m, j)
+    for h in range(2):
+        pushes[4 + h].wait_recv()
+        for j in chunks(h):
+            for c in range(j * NC // NJ, (j + 1) * NC // NJ):
+                down(c)
+            for m in (8, 7):
+                pass_on(m, j)
     for m in (5, 6, 3, 4, 1, 2):
         for j in range(NJ):
             pass_on(m, j)

time: 60.4 us -> 59.7 us (0.988)
  Pallas kernels: 58.9 us -> 58.2 us
    pallas_call x1, Pallas kernels: 58.9 us -> 58.2 us  [local(): pl.pallas_call(kernel, out_shape=pltpu.VMEM((8, D), bf16), in_specs=[hbm]...]
where the time goes in v6:
time: 59.7 us; the launch traced here: 59.5 us
  Pallas kernels  58.2 us (97%)
  local copies, waits for them, and re-layouts  0.69 us (1%)
  between operations  0.66 us (1%)
    pallas_call x1, Pallas kernels, local(): pl.pallas_call(kernel, out_shape=pltpu.VMEM((8, D), bf16), in_specs=[hbm]...  58.2 us

profile of v6, /device:TPU:24, one launch (start us, length us, event | category | flops | bytes accessed | tf_op | source)
XLA Modules:
  0.0 59.5 jit_solution(14062068663507606793)
XLA Ops:
  0.7 58.2 %shard_map.127 = bf16[8,4096]{1,0:T(8,128)(2,1)S(1)} custom-call(s32[1]{0:T(128)S(6)} %copy.14.bs_in, s32[2]{0:T(128)} %cl_in.1, s32[2,16]{1,0:T(2,128)} %pt_in.1, bf16[4,2,4096]{2,1,0:T(2,128)(2,1)} %li_ref.1, bf16[4,2,4096]{2,1,0:T(2,128)(2,1)} %q_ref.1, bf16[4,2,512]{2,1,0:T(2,128)(2,1)} %nk_ref.1, bf16[4,2,512]{2,1,0:T(2,128)(2,1)} %nv_ref.1, ...), custom_call_target="tpu_custom_call" | custom-call | tf_op jit(solution)/shard_map/pallas_call | solution.py:370
  58.9 0.7 %reshape.15 = bf16[4,2,4096]{2,1,0:T(2,128)(2,1)} reshape(bf16[8,4096]{1,0:T(8,128)(2,1)S(1)} %shard_map.127) | data formatting | bytes 131072 | tf_op jit(solution)/shard_map/reshape | solution.py:426

commit v7 on v6

--- a/solution.py
+++ b/solution.py
@@ -109,13 +109,18 @@
     def lanes(j):
         return pl.ds(j * W, W)
 
-    def sent_lanes(j):
-        return pl.ds(j * W, W + SCALE if j == NJ - 1 else W)
-
-    def ag(src, dst, j, dev):
+    def parts(m):
+        return 2 if m % 2 else NJ
+
+    def part_lanes(m, j):
+        size = HALF // parts(m)
+        return pl.ds(j * size, size)
+
+    def ag(src, dst, m, j, dev):
+        size = HALF // parts(m)
+        part = pl.ds(j * size, size + SCALE if j == parts(m) - 1 else size)
         return remote(
-            gath.at[src, :, sent_lanes(j)], gath.at[dst, :, sent_lanes(j)],
-            ag_send.at[0], ag_recv.at[dst, j], dev,
+            gath.at[src, :, part], gath.at[dst, :, part], ag_send.at[0], ag_recv.at[dst, j], dev
         )
 
     def chunks(h):
@@ -126,14 +131,17 @@
 
     def spread(m, j):
         for n in children(m):
+            if n % 2 and j % 2 == 0:
+                continue
+            part = j // 2 if n % 2 else j
             for sign, devices in ((1, right), (-1, left)):
                 if goes(n, j, sign):
-                    ag(slot_of(-sign * m), slot_of(-sign * n), j, devices[n - m]).start()
+                    ag(slot_of(-sign * m), slot_of(-sign * n), n, part, devices[n - m]).start()
 
     def arrive(m, j):
         for sign in (1, -1):
             if goes(m, j, sign):
-                ag(0, slot_of(-sign * m), j, right[1]).wait_recv()
+                ag(0, slot_of(-sign * m), m, j, right[1]).wait_recv()
 
     def stacked(ref, width):
         for s in range(4):
@@ -280,13 +288,13 @@
 
     def plus(m, j):
         return remote(
-            sp.at[m - 1, :, lanes(j)], rp.at[m - 1, :, lanes(j)],
+            sp.at[m - 1, :, part_lanes(m, j)], rp.at[m - 1, :, part_lanes(m, j)],
             ps_send.at[m // 8], ps_recv.at[m - 1, j], right[m - PARENT[m]],
         )
 
     def minus(m, j):
         return remote(
-            sm.at[m - 1, :, lanes(j)], rm.at[m - 1, :, lanes(j)],
+            sm.at[m - 1, :, part_lanes(m, j)], rm.at[m - 1, :, part_lanes(m, j)],
             ms_send.at[m // 8], ms_recv.at[m - 1, j], left[m - PARENT[m]],
         )
 
@@ -296,24 +304,28 @@
         for sign, copy, leaving, arrived in sides:
             if not goes(m, j, sign):
                 continue
-            slot = slot_of(sign * m)
-            value = own[slot, :, lanes(j)]
+            here = part_lanes(m, j)
+            value = own[slot_of(sign * m), :, here]
             for source in children(m):
-                if goes(source, j, sign):
+                if not goes(source, j, sign):
+                    continue
+                if source % 2 == 0:
                     copy(source, j).wait_recv()
-                    value = value + arrived[source - 1, :, lanes(j)].astype(jnp.float32)
-            leaving[m - 1, :, lanes(j)] = value.astype(jnp.bfloat16)
+                elif j % 2 == 0:
+                    copy(source, j // 2).wait_recv()
+                value = value + arrived[source - 1, :, here].astype(jnp.float32)
+            leaving[m - 1, :, here] = value.astype(jnp.bfloat16)
             copy(m, j).start()
 
     for m in (2, 1, 4, 3, 6, 5):
-        for j in range(NJ):
+        for j in range(parts(m)):
             arrive(m, j)
             spread(m, j)
     for name in ("wg", "wu"):
         loads[name].wait()
     for h in range(2):
+        arrive(7, h)
         for j in chunks(h):
-            arrive(7, j)
             arrive(8, j)
         for push in pushes[2 * h : 2 * h + 2]:
             push.wait_recv()
@@ -325,17 +337,29 @@
         for j in chunks(h):
             for c in range(j * NC // NJ, (j + 1) * NC // NJ):
                 down(c)
-            for m in (8, 7):
-                pass_on(m, j)
+            pass_on(8, j)
+        pass_on(7, h)
     for m in (5, 6, 3, 4, 1, 2):
-        for j in range(NJ):
+        for j in range(parts(m)):
             pass_on(m, j)
+
+    def sent(part, sem):
+        remote(part, part, sem, sem, sib).wait_send()
+
+    for push in pushes:
+        push.wait_send()
+    sent(gath.at[pl.ds(1, 15)], ag_send.at[0])
+    sent(sp.at[7, :, pl.ds(0, HALF // 2)], ps_send.at[1])
+    sent(sm.at[7, :, pl.ds(0, HALF // 2)], ms_send.at[1])
+    sent(sp.at[pl.ds(0, 7)], ps_send.at[0])
+    sent(sm.at[pl.ds(0, 7)], ms_send.at[0])
 
     alive = jnp.bitwise_and(lax.broadcasted_iota(jnp.int32, (8, CW), 0), 1) < bs[0]
     for j in range(NJ):
         for m in children(0):
-            plus(m, j).wait_recv()
-            minus(m, j).wait_recv()
+            if m % 2 == 0 or j % 2 == 0:
+                plus(m, j // 2 if m % 2 else j).wait_recv()
+                minus(m, j // 2 if m % 2 else j).wait_recv()
         for c in range(j * NC // NJ, (j + 1) * NC // NJ):
             value = own[0, :, piece(c)]
             for m in children(0):
@@ -345,17 +369,6 @@
                 place = pl.ds((2 * c + fold) * CW, CW)
                 done = res[:, place] + value[8 * fold : 8 * fold + 8]
                 out_ref[:, place] = jnp.where(alive, done, 0.0).astype(jnp.bfloat16)
-
-    def sent(part, sem):
-        remote(part, part, sem, sem, sib).wait_send()
-
-    for push in pushes:
-        push.wait_send()
-    sent(gath.at[pl.ds(1, 15)], ag_send.at[0])
-    sent(sp.at[7, :, pl.ds(0, HALF // 2)], ps_send.at[1])
-    sent(sm.at[7, :, pl.ds(0, HALF // 2)], ms_send.at[1])
-    sent(sp.at[pl.ds(0, 7)], ps_send.at[0])
-    sent(sm.at[pl.ds(0, 7)], ms_send.at[0])
 
 
 def local(

time: 59.7 us -> 59.6 us (level)
  no operation moved by 1% of the time
where the time goes in v7:
time: 59.6 us; the launch traced here: 59.1 us
  Pallas kernels  57.8 us (97%)
  local copies, waits for them, and re-layouts  0.69 us (1%)
  between operations  0.66 us (1%)
    pallas_call x1, Pallas kernels, local(): pl.pallas_call(kernel, out_shape=pltpu.VMEM((8, D), bf16), in_specs=[hbm]...  57.8 us

profile of v7, /device:TPU:24, one launch (start us, length us, event | category | flops | bytes accessed | tf_op | source)
XLA Modules:
  0.0 59.1 jit_solution(12072620786919951972)
XLA Ops:
  0.7 57.8 %shard_map.127 = bf16[8,4096]{1,0:T(8,128)(2,1)S(1)} custom-call(s32[1]{0:T(128)S(6)} %copy.14.bs_in, s32[2]{0:T(128)} %cl_in.1, s32[2,16]{1,0:T(2,128)} %pt_in.1, bf16[4,2,4096]{2,1,0:T(2,128)(2,1)} %li_ref.1, bf16[4,2,4096]{2,1,0:T(2,128)(2,1)} %q_ref.1, bf16[4,2,512]{2,1,0:T(2,128)(2,1)} %nk_ref.1, bf16[4,2,512]{2,1,0:T(2,128)(2,1)} %nv_ref.1, ...), custom_call_target="tpu_custom_call" | custom-call | tf_op jit(solution)/shard_map/pallas_call | solution.py:383
  58.5 0.7 %reshape.15 = bf16[4,2,4096]{2,1,0:T(2,128)(2,1)} reshape(bf16[8,4096]{1,0:T(8,128)(2,1)S(1)} %shard_map.127) | data formatting | bytes 131072 | tf_op jit(solution)/shard_map/reshape | solution.py:439

commit v8 on v7

--- a/solution.py
+++ b/solution.py
@@ -317,7 +317,7 @@
             leaving[m - 1, :, here] = value.astype(jnp.bfloat16)
             copy(m, j).start()
 
-    for m in (2, 1, 4, 3, 6, 5):
+    for m in (2, 4, 6, 1, 3, 5):
         for j in range(parts(m)):
             arrive(m, j)
             spread(m, j)

time: 59.6 us -> 59.6 us (level)
  no operation moved by 1% of the time
where the time goes in v8:
time: 59.6 us; the launch traced here: 59.1 us
  Pallas kernels  57.8 us (97%)
  local copies, waits for them, and re-layouts  0.69 us (1%)
  between operations  0.66 us (1%)
    pallas_call x1, Pallas kernels, local(): pl.pallas_call(kernel, out_shape=pltpu.VMEM((8, D), bf16), in_specs=[hbm]...  57.8 us

profile of v8, /device:TPU:24, one launch (start us, length us, event | category | flops | bytes accessed | tf_op | source)
XLA Modules:
  0.0 59.1 jit_solution(12168930490624296736)
XLA Ops:
  0.7 57.8 %shard_map.127 = bf16[8,4096]{1,0:T(8,128)(2,1)S(1)} custom-call(s32[1]{0:T(128)S(6)} %copy.14.bs_in, s32[2]{0:T(128)} %cl_in.1, s32[2,16]{1,0:T(2,128)} %pt_in.1, bf16[4,2,4096]{2,1,0:T(2,128)(2,1)} %li_ref.1, bf16[4,2,4096]{2,1,0:T(2,128)(2,1)} %q_ref.1, bf16[4,2,512]{2,1,0:T(2,128)(2,1)} %nk_ref.1, bf16[4,2,512]{2,1,0:T(2,128)(2,1)} %nv_ref.1, ...), custom_call_target="tpu_custom_call" | custom-call | tf_op jit(solution)/shard_map/pallas_call | solution.py:383
  58.5 0.7 %reshape.15 = bf16[4,2,4096]{2,1,0:T(2,128)(2,1)} reshape(bf16[8,4096]{1,0:T(8,128)(2,1)S(1)} %shard_map.127) | data formatting | bytes 131072 | tf_op jit(solution)/shard_map/reshape | solution.py:439

commit v9 on v7

--- a/solution.py
+++ b/solution.py
@@ -174,6 +174,7 @@
         & (lax.shift_right_arithmetic(col8, 1) <= lax.shift_right_logical(row8, 1))
     )
     bias = jnp.where(fresh, 0.0, bias)
+    bias = jnp.concatenate([bias] * 16, 0).T
 
     loads["q"].wait()
     qf = stacked(q, D)
@@ -200,16 +201,15 @@
         these = slice(2 * pair * HD, 2 * (pair + 1) * HD)
         loads[("k0", "k1")[pair]].wait()
         scores = lax.dot_general(
-            both, kb[:, these], (((1,), (1,)), ((), ())), preferred_element_type=jnp.float32
-        )
-        scores = (scores.reshape(16, 8, KEYS) * scale + bias[None]).reshape(128, KEYS)
-        highest = jnp.max(scores, axis=-1, keepdims=True)
-        expo = jnp.exp(scores - highest)
-        total = jnp.sum(expo, axis=-1, keepdims=True)
+            kb[:, these], both, (((1,), (1,)), ((), ())), preferred_element_type=jnp.float32
+        )
+        scores = scores * scale + bias
+        expo = jnp.exp(scores - jnp.max(scores, axis=0, keepdims=True))
+        weights = expo * (1.0 / jnp.sum(expo, axis=0, keepdims=True))
         loads[("v0", "v1")[pair]].wait()
         mixed = jnp.dot(
-            expo.astype(jnp.bfloat16), vb[:, these], preferred_element_type=jnp.float32
-        ) / total
+            weights.T.astype(jnp.bfloat16), vb[:, these], preferred_element_type=jnp.float32
+        )
         attention = jnp.concatenate(
             [
                 mixed[64 * i + 8 * g : 64 * i + 8 * g + 8, i * HD : (i + 1) * HD]

time: 59.6 us -> 60.1 us (level)
    pallas_call x1, Pallas kernels: 57.8 us -> 58.4 us  [local(): pl.pallas_call(kernel, out_shape=pltpu.VMEM((8, D), bf16), in_specs=[hbm]...]
where the time goes in v9:
time: 60.1 us; the launch traced here: 59.7 us
  Pallas kernels  58.4 us (97%)
  local copies, waits for them, and re-layouts  0.69 us (1%)
  between operations  0.66 us (1%)
    pallas_call x1, Pallas kernels, local(): pl.pallas_call(kernel, out_shape=pltpu.VMEM((8, D), bf16), in_specs=[hbm]...  58.4 us

profile of v9, /device:TPU:24, one launch (start us, length us, event | category | flops | bytes accessed | tf_op | source)
XLA Modules:
  0.0 59.7 jit_solution(15443748535717060707)
XLA Ops:
  0.7 58.4 %shard_map.127 = bf16[8,4096]{1,0:T(8,128)(2,1)S(1)} custom-call(s32[1]{0:T(128)S(6)} %copy.14.bs_in, s32[2]{0:T(128)} %cl_in.1, s32[2,16]{1,0:T(2,128)} %pt_in.1, bf16[4,2,4096]{2,1,0:T(2,128)(2,1)} %li_ref.1, bf16[4,2,4096]{2,1,0:T(2,128)(2,1)} %q_ref.1, bf16[4,2,512]{2,1,0:T(2,128)(2,1)} %nk_ref.1, bf16[4,2,512]{2,1,0:T(2,128)(2,1)} %nv_ref.1, ...), custom_call_target="tpu_custom_call" | custom-call | tf_op jit(solution)/shard_map/pallas_call | solution.py:383
  59.1 0.7 %reshape.15 = bf16[4,2,4096]{2,1,0:T(2,128)(2,1)} reshape(bf16[8,4096]{1,0:T(8,128)(2,1)S(1)} %shard_map.127) | data formatting | bytes 131072 | tf_op jit(solution)/shard_map/reshape | solution.py:439

commit v10 on v7

--- a/solution.py
+++ b/solution.py
@@ -339,7 +339,7 @@
                 down(c)
             pass_on(8, j)
         pass_on(7, h)
-    for m in (5, 6, 3, 4, 1, 2):
+    for m in (5, 6, 3, 1, 4, 2):
         for j in range(parts(m)):
             pass_on(m, j)
 

time: 59.6 us -> 59.7 us (level)
  no operation moved by 1% of the time
where the time goes in v10:
time: 59.7 us; the launch traced here: 59.3 us
  Pallas kernels  58 us (97%)
  local copies, waits for them, and re-layouts  0.69 us (1%)
  between operations  0.66 us (1%)
    pallas_call x1, Pallas kernels, local(): pl.pallas_call(kernel, out_shape=pltpu.VMEM((8, D), bf16), in_specs=[hbm]...  58 us

profile of v10, /device:TPU:24, one launch (start us, length us, event | category | flops | bytes accessed | tf_op | source)
XLA Modules:
  0.0 59.3 jit_solution(16023009181078545843)
XLA Ops:
  0.7 58.0 %shard_map.127 = bf16[8,4096]{1,0:T(8,128)(2,1)S(1)} custom-call(s32[1]{0:T(128)S(6)} %copy.14.bs_in, s32[2]{0:T(128)} %cl_in.1, s32[2,16]{1,0:T(2,128)} %pt_in.1, bf16[4,2,4096]{2,1,0:T(2,128)(2,1)} %li_ref.1, bf16[4,2,4096]{2,1,0:T(2,128)(2,1)} %q_ref.1, bf16[4,2,512]{2,1,0:T(2,128)(2,1)} %nk_ref.1, bf16[4,2,512]{2,1,0:T(2,128)(2,1)} %nv_ref.1, ...), custom_call_target="tpu_custom_call" | custom-call | tf_op jit(solution)/shard_map/pallas_call | solution.py:383
  58.6 0.7 %reshape.15 = bf16[4,2,4096]{2,1,0:T(2,128)(2,1)} reshape(bf16[8,4096]{1,0:T(8,128)(2,1)S(1)} %shard_map.127) | data formatting | bytes 131072 | tf_op jit(solution)/shard_map/reshape | solution.py:439
